TPU v7x, 32 devices: a whole 2x2x4 slice. The times are simulated.
32 devices in a mesh: row: 4 (over z), col: 8 (over y, x, core).
Axes of the slice: x: 2, y: 2, z: 4, core: 2. Of those that a mesh axis runs over, the one named last changes fastest.
Arguments:
- t_amps: bfloat16 [3, 4096, 4096], P(None, ('row', 'col')), may hold values from -0.099609375 to 0.099609375
- w_cycle: bfloat16 [3, 4096, 4096], P(None, ('row', 'col')), may hold values from -3 to 3
- v_cycle: bfloat16 [3, 4096, 4096], P(None, ('row', 'col')), may hold values from -6 to 6
- occ_irrep: int32 [50], replicated, may hold values from 0 to 7, as said below
- vir_irrep: int32 [500], replicated, may hold values from 0 to 7, as said below
- e_occ: float32 [50], replicated, may hold values from -2.5 to -0.5
- e_vir: float32 [500], replicated, may hold values from 0.5 to 3
Outputs:
- t_new: float32 [3, 4096, 4096], P(None, ('row', 'col'))
Inputs may be any that keep to these rules, and one draw needn't show every extreme that they name: `occ_irrep`: a random permutation of a label table in which irrep h holds floor(50 * c_h / 50) - floor(50 * c_(h-1) / 50) orbitals, with cumulative c = 12, 16, 24, 29, 33, 39, 45, 50 for h = 0 to 7. `vir_irrep`: a random permutation of a label table in which irrep h holds floor(500 * c_h / 500) - floor(500 * c_(h-1) / 500) orbitals, with cumulative c = 100, 145, 220, 275, 315, 380, 445, 500 for h = 0 to 7.
All inputs are finite; a program needn't handle non-finite values.
Results may differ from a plain program's by a relative error of at most 0.0035.
Values may be sent and summed in bfloat16 or wider, within the bound.
A program may use at most 192 MiB of HBM per device.

v0:
```python
import jax
import jax.numpy as jnp
from jax import lax
from jax.sharding import PartitionSpec as P


def pair_table(occ_irrep, vir_irrep, e_occ, e_vir, blocks, slots):
    sym = jnp.bitwise_xor(vir_irrep[:, None], occ_irrep[None, :]).reshape(-1)
    energy = (e_occ[None, :] - e_vir[:, None]).reshape(-1)
    tables = []
    counts = []
    for group in range(blocks):
        hit = (sym == group).astype(jnp.int32)
        rank = jnp.cumsum(hit) - 1
        target = jnp.where(hit > 0, rank, slots)
        tables.append(jnp.full((slots,), -1.0, jnp.float32).at[target].set(energy, mode="drop"))
        counts.append(jnp.sum(hit))
    return (jnp.stack(tables), jnp.stack(counts))


def body(t_amps, w_cycle, v_cycle, occ_irrep, vir_irrep, e_occ, e_vir):
    blocks, own_rows, slots = t_amps.shape
    device = lax.axis_index(("row", "col"))
    pair_energy, counts = pair_table(occ_irrep, vir_irrep, e_occ, e_vir, blocks, slots)
    slot = jnp.arange(slots, dtype=jnp.int32)
    alive = slot[None, :] < counts[:, None]
    row_alive = lax.dynamic_slice_in_dim(alive, device * own_rows, own_rows, 1)
    live = row_alive[:, :, None] & alive[:, None, :]
    zero_half = jnp.zeros((), jnp.bfloat16)
    tm = jnp.where(live, t_amps, zero_half)
    wm = jnp.where(live, w_cycle, zero_half)
    vm = jnp.where(live, v_cycle, zero_half)
    t_grid, w_grid, v_grid = (
        lax.all_to_all(tm, "col", split_axis=2, concat_axis=1, tiled=True),
        lax.all_to_all(wm, "col", split_axis=2, concat_axis=1, tiled=True),
        lax.all_to_all(vm, "col", split_axis=2, concat_axis=1, tiled=True),
    )
    v_panel = lax.all_gather(v_grid, "col", axis=2, tiled=True)
    left = v_panel
    product = jnp.einsum(
        "gik,gkj->gij",
        left,
        lax.all_gather(t_grid, "row", axis=1, tiled=True),
        preferred_element_type=jnp.float32,
    )
    x_grid = (w_grid.astype(jnp.float32) + 0.5 * product).astype(jnp.bfloat16)
    t_panel = lax.all_gather(t_grid, "col", axis=2, tiled=True)
    left = t_panel
    z_grid = jnp.einsum(
        "gik,gkj->gij",
        left,
        lax.all_gather(x_grid, "row", axis=1, tiled=True),
        preferred_element_type=jnp.float32,
    )
    z_rows = lax.all_to_all(
        z_grid.astype(jnp.bfloat16), "col", split_axis=1, concat_axis=2, tiled=True
    ).astype(z_grid.dtype)
    flipped = jnp.transpose(z_rows, (0, 2, 1))
    z_mirror = lax.all_to_all(
        flipped.astype(jnp.bfloat16), ("row", "col"), split_axis=1, concat_axis=2, tiled=True
    ).astype(flipped.dtype)
    row_energy = lax.dynamic_slice_in_dim(pair_energy, device * own_rows, own_rows, 1)
    denom = row_energy[:, :, None] + pair_energy[:, None, :]
    numer = vm.astype(jnp.float32) + z_rows + z_mirror
    return jnp.where(live, numer / denom, jnp.zeros((), jnp.float32))


def solution(mesh):
    in_specs = (
        P(None, ("row", "col"), None),
        P(None, ("row", "col"), None),
        P(None, ("row", "col"), None),
        P(),
        P(),
        P(),
        P(),
    )
    out_specs = P(None, ("row", "col"), None)
    return jax.shard_map(body, mesh=mesh, in_specs=in_specs, out_specs=out_specs, check_vma=False)
```

profile of v0, /device:TPU:0, one launch (start us, length us, event | category | flops | bytes accessed | tf_op | source)
XLA Modules:
  0.0 1292.9 jit_solution(18280217707633101036)
XLA Ops:
  6.5 1.6 fusion.10
  8.1 2.0 pad_add_fusion
  10.1 0.3 iota_compare_fusion
  10.6 7.3 copy.57
  17.8 7.2 copy.58
  25.0 7.1 copy.60
  32.1 16.5 %and_select_fusion.3 = (bf16[3,128,4096]{1,0,2:T(4,128)(2,1)}, bf16[3,128,4096]{1,0,2:T(4,128)(2,1)}, bf16[3,128,4096]{1,0,2:T(4,128)(2,1)S(1)}) fusion(bf16[3,128,4096]{1,0,2:T(4,128)(2,1)} %copy.57, pred[3,4096]{0,1:T(8,128)(4,1)S(1)} %iota_compare_fusion, pred[3,128]{1,0:T(4,128)(4,1)S(1)} %copy.56, bf16[3,128,4096]{1,0,2:T(4,128)(2,1)} %copy.60, ...), kind=kLoop, calls=%fused_computation.6 | loop fusion | flops 6291456 | bytes 18887040 | tf_op jit(solution)/shard_map/jit(_where)/select_n | solution.py:32
  48.6 54.1 %all_to_all.63 = bf16[3,128,4096]{1,0,2:T(4,128)(2,1)} all-to-all(bf16[3,128,4096]{1,0,2:T(4,128)(2,1)S(1)} %get-tuple-element.10), channel_id=1, replica_groups=mesh['row'=4,'col'=8] {'col'}, dimensions={2} | all-to-all | bytes 6291456 | tf_op jit(solution)/shard_map/all_to_all | solution.py:34
  102.8 7.1 copy.59
  109.9 52.7 %all_to_all.64 = bf16[3,128,4096]{1,0,2:T(4,128)(2,1)S(1)} all-to-all(bf16[3,128,4096]{1,0,2:T(4,128)(2,1)} %get-tuple-element.8), channel_id=1, replica_groups=mesh['row'=4,'col'=8] {'col'}, dimensions={2} | all-to-all | bytes 6291456 | tf_op jit(solution)/shard_map/all_to_all | solution.py:36
  162.6 0.5 copy.62
  163.1 2.9 copy.63
  166.0 0.7 all-gather.5.cloned.1.call-update
  166.7 53.6 %all_to_all.65 = bf16[3,128,4096]{1,0,2:T(4,128)(2,1)} all-to-all(bf16[3,128,4096]{1,0,2:T(4,128)(2,1)} %get-tuple-element.9), channel_id=1, replica_groups=mesh['row'=4,'col'=8] {'col'}, dimensions={2} | all-to-all | bytes 6291456 | tf_op jit(solution)/shard_map/all_to_all | solution.py:35
  220.3 7.9 copy.61
  228.2 99.5 %all-gather.9.cloned.1.call-done = bf16[3,4096,512]{2,1,0:T(8,128)(2,1)} async-done(((bf16[3,1024,512]{2,1,0:T(8,128)(2,1)}), bf16[3,4096,512]{2,1,0:T(8,128)(2,1)}) %all-gather.9.cloned.1.call-update) | async-done | bytes 12582928 | tf_op jit(solution)/shard_map/all_gather | solution.py:43
  327.6 130.4 %all-gather.7.cloned.1.call-done = bf16[3,1024,4096]{2,1,0:T(8,128)(2,1)} async-done(((bf16[3,1024,512]{2,1,0:T(8,128)(2,1)}), bf16[3,1024,4096]{2,1,0:T(8,128)(2,1)}) %all-gather.7.cloned.1.call-update) | async-done | bytes 25165840 | tf_op jit(solution)/shard_map/all_gather | solution.py:38
  458.0 24.1 %fusion.1 = bf16[3,1024,512]{2,1,0:T(8,128)(2,1)} fusion(f32[3,128,8,512]{3,1,2,0:T(8,128)} %copy.61, bf16[3,1024,4096]{2,1,0:T(8,128)(2,1)} %all-gather.7.cloned.1.call-done, bf16[3,4096,512]{2,1,0:T(8,128)(2,1)} %all-gather.9.cloned.1.call-done), kind=kOutput, calls=%fused_computation.10 | convolution fusion | flops 12889620480 | bytes 47185920 | tf_op jit(solution)/shard_map/gik,gkj->gij/dot_general | solution.py:40
  482.1 108.1 %all-gather.5.cloned.1.call-done = bf16[3,1024,4096]{2,1,0:T(8,128)(2,1)} async-done(((bf16[3,1024,512]{2,1,0:T(8,128)(2,1)}), bf16[3,1024,4096]{2,1,0:T(8,128)(2,1)}) %all-gather.5.cloned.1.call-update) | async-done | bytes 25165840 | tf_op jit(solution)/shard_map/all_gather | solution.py:47
  590.2 219.7 %all-gather.11.cloned.1.call-done = bf16[3,4096,512]{2,1,0:T(8,128)(2,1)} async-done(((bf16[3,1024,512]{2,1,0:T(8,128)(2,1)}), bf16[3,4096,512]{2,1,0:T(8,128)(2,1)}) %all-gather.11.cloned.1.call-update) | async-done | bytes 12582928 | tf_op jit(solution)/shard_map/all_gather | solution.py:52
  809.8 21.5 %convolution_convert_fusion = bf16[3,1024,512]{2,1,0:T(8,128)(2,1)S(1)} fusion(bf16[3,1024,4096]{2,1,0:T(8,128)(2,1)} %all-gather.5.cloned.1.call-done, bf16[3,4096,512]{2,1,0:T(8,128)(2,1)} %all-gather.11.cloned.1.call-done), kind=kOutput, calls=%fused_computation.11 | convolution fusion | flops 12886474752 | bytes 40894464 | tf_op jit(solution)/shard_map/gik,gkj->gij/dot_general | solution.py:49
  831.3 4.7 copy.64
  836.0 4.9 all-to-all-start.3
  841.0 0.1 fusion.2
  841.1 0.2 reshape.141
  841.4 0.2 reduce-window.40
  841.6 48.2 %all-to-all-done.3 = bf16[3,1024,512]{2,0,1:T(4,128)(2,1)} async-done(((bf16[3,1024,512]{2,0,1:T(4,128)(2,1)}), bf16[3,1024,512]{2,0,1:T(4,128)(2,1)}, u32[]{:S(2)}, u32[]{:S(2)}) %all-to-all-start.3) | async-done | bytes 3145760 | tf_op jit(solution)/shard_map/all_to_all | solution.py:55
  889.9 10.0 copy.65
  899.9 3.7 all-to-all-start.4
  903.6 0.3 reduce-window.41
  904.0 0.1 slice_reduce_fusion.2
  904.4 0.1 broadcast_subtract_fusion
  904.6 0.2 reshape.166
  904.8 0.2 reshape.142
  905.1 0.2 reduce-window.54
  905.3 0.3 reduce-window.55
  905.7 0.1 slice_reduce_fusion.1
  906.1 115.2 %scatter_custom_fusion = f32[4096]{0:T(1024)S(1)} fusion(s32[25000]{0:T(1024)S(1)} %compare_select_fusion.2, f32[25000]{0:T(1024)S(1)} %reshape.166, f32[]{:T(128)} %constant.36.clone.1), kind=kCustom, calls=%fused_computation.43 | custom fusion | bytes 16388 | tf_op jit(solution)/shard_map/scatter | solution.py:16
  1021.4 115.2 %scatter_custom_fusion.1 = f32[4096]{0:T(1024)S(1)} fusion(s32[25000]{0:T(1024)S(1)} %compare_select_fusion.1, f32[25000]{0:T(1024)S(1)} %reshape.166, f32[]{:T(128)} %constant.36.clone.1), kind=kCustom, calls=%fused_computation.41 | custom fusion | bytes 16388 | tf_op jit(solution)/shard_map/scatter | solution.py:16
  1136.6 0.2 reshape.143
  1136.9 0.2 reduce-window.57
  1137.1 0.3 reduce-window.58
  1137.6 0.1 slice_reduce_fusion
  1138.0 115.2 %scatter_custom_fusion.2 = f32[4096]{0:T(1024)S(1)} fusion(s32[25000]{0:T(1024)S(1)} %compare_select_fusion, f32[25000]{0:T(1024)S(1)} %reshape.166, f32[]{:T(128)} %constant.36.clone.1), kind=kCustom, calls=%fused_computation.39 | custom fusion | bytes 16388 | tf_op jit(solution)/shard_map/scatter | solution.py:16
  1253.3 0.6 copy.73
  1253.9 9.9 copy.66
  1263.9 13.5 %and_select_fusion = f32[3,128,4096]{1,0,2:T(4,128)} fusion(f32[3,32,128,128]{2,0,3,1:T(4,128)} %copy.66, bf16[3,8,128,512]{2,0,3,1:T(4,128)(2,1)} %copy.65, f32[3,4096]{0,1:T(8,128)S(1)} %copy.73, f32[3,128]{1,0:T(4,128)S(1)} %constant_dynamic-slice_fusion, pred[3,4096]{0,1:T(8,128)(4,1)S(1)} %copy-done.1, pred[3,128]{1,0:T(4,128)(4,1)S(1)} %copy.56, ...), kind=kLoop, calls=%fused_computation.3 | loop fusion | flops 14155776 | bytes 18937728 | tf_op jit(solution)/shard_map/jit(_where)/select_n | solution.py:65
  1277.4 9.0 copy.74
  (57 shorter events, 1.9 us)
Async XLA Ops:
  6.5 321.1 %all-gather.9.cloned.1.call-start = ((), (), s32[]{:S(2)}) async-start(), calls=%async_computation.7 | async-start | bytes 15728640 | tf_op jit(solution)/shard_map/all_gather | solution.py:43
  10.4 21.7 %copy-start = (pred[3,4096]{0,1:T(8,128)(4,1)}, pred[3,4096]{0,1:T(8,128)(4,1)S(1)}, u32[]{:S(2)}) copy-start(pred[3,4096]{0,1:T(8,128)(4,1)S(1)} %iota_compare_fusion) | copy-start | bytes 36868
  109.9 348.1 %all-gather.7.cloned.1.call-start = ((), (), s32[]{:S(2)}) async-start(), calls=%async_computation.6 | async-start | bytes 28311552 | tf_op jit(solution)/shard_map/all_gather | solution.py:38
  166.0 424.2 %all-gather.5.cloned.1.call-start = ((), (), s32[]{:S(2)}) async-start(), calls=%async_computation.5 | async-start | bytes 28311552 | tf_op jit(solution)/shard_map/all_gather | solution.py:47
  166.7 643.1 %all-gather.11.cloned.1.call-start = ((), (), s32[]{:S(2)}) async-start(), calls=%async_computation.8 | async-start | bytes 15728640 | tf_op jit(solution)/shard_map/all_gather | solution.py:52
  836.0 4.9 copy-start.2
  836.0 4.9 copy-start.4
  836.0 53.8 %all-to-all-start.3 = ((bf16[3,1024,512]{2,0,1:T(4,128)(2,1)}), bf16[3,1024,512]{2,0,1:T(4,128)(2,1)}, u32[]{:S(2)}, u32[]{:S(2)}) async-start(bf16[3,1024,512]{2,0,1:T(4,128)(2,1)} %copy.64), calls=%async_computation.3 | async-start | bytes 8388608 | tf_op jit(solution)/shard_map/all_to_all | solution.py:55
  899.8 4.5 copy-start.3
  899.9 4.6 copy-start.5
  899.9 354.1 %all-to-all-start.4 = ((bf16[3,4096,128]{2,0,1:T(4,128)(2,1)}), bf16[3,4096,128]{2,0,1:T(4,128)(2,1)}, u32[]{:S(2)}, u32[]{:S(2)}) async-start(bf16[3,4096,128]{2,0,1:T(4,128)(2,1)} %bitcast.70), calls=%async_computation.4 | async-start | bytes 8388608 | tf_op jit(solution)/shard_map/all_to_all | solution.py:59
  1253.9 9.9 copy-start.1
Sparse Core Ops, SparseCore 0:
  110.0 217.5 all-gather.8
  329.5 128.4 all-gather.6
  459.9 130.2 all-gather.4
  591.6 218.1 all-gather.10
where the time goes:
time: 1290 us
  waiting for transfers between devices  607 us (47%)
  local copies, waits for them, and re-layouts  422 us (33%)
  blocking collectives  160 us (12%)
  matrix products  45.6 us (4%)
  other arithmetic  36.2 us (3%)
  between operations  13.5 us (1%)
    scatter x3, local copies, waits for them, and re-layouts, pair_table(): jnp.full((slots,), -1.0, jnp.float32).at[target].set(energy, mode='drop')  346 us
    all_gather x1, waiting for transfers between devices, body(): lax.all_gather(x_grid, 'row', axis=1, tiled=True)  220 us
    all_gather x1, waiting for transfers between devices, body(): v_panel = lax.all_gather(v_grid, 'col', axis=2, tiled=True)  130 us
    all_gather x1, waiting for transfers between devices, body(): t_panel = lax.all_gather(t_grid, 'col', axis=2, tiled=True)  108 us
    all_gather x1, waiting for transfers between devices, body(): lax.all_gather(t_grid, 'row', axis=1, tiled=True)  99.5 us
    all_to_all x1, blocking collectives, body(): lax.all_to_all(tm, 'col', split_axis=2, concat_axis=1, tiled=True)  54.1 us
    all_to_all x1, blocking collectives, body(): lax.all_to_all(wm, 'col', split_axis=2, concat_axis=1, tiled=True)  53.6 us
    all_to_all x1, blocking collectives, body(): lax.all_to_all(vm, 'col', split_axis=2, concat_axis=1, tiled=True)  52.7 us
  transfers between devices with their start and end apart: 6, of which 5 were waited for; matrix products, arithmetic and copies ran while one was open for 30% of the time, Pallas kernels for 0%

commit v1 on v0

v1 whole, which is shorter than its diff:
```python
import functools

import jax
import jax.numpy as jnp
from jax import lax
from jax.experimental import pallas as pl
from jax.experimental.pallas import tpu as pltpu
from jax.sharding import PartitionSpec as P

OCC_CUM = (12, 16, 24, 29, 33, 39, 45, 50)
VIR_CUM = (100, 145, 220, 275, 315, 380, 445, 500)
MESH = pl.DeviceIdType.MESH


def block_counts(n_occ, n_vir, blocks):
    occ = [n_occ * c // 50 for c in OCC_CUM]
    vir = [n_vir * c // 500 for c in VIR_CUM]
    occ = [b - a for a, b in zip([0] + occ, occ)]
    vir = [b - a for a, b in zip([0] + vir, vir)]
    return [sum(occ[h] * vir[h ^ g] for h in range(8)) for g in range(blocks)]


def pair_table(occ_irrep, vir_irrep, e_occ, e_vir, counts, slots):
    blocks = len(counts)
    n_occ = occ_irrep.shape[0]
    group = jnp.arange(blocks, dtype=jnp.int32)
    want = jnp.bitwise_xor(vir_irrep[None, :], group[:, None])
    per = jnp.sum((want[:, :, None] == occ_irrep[None, None, :]).astype(jnp.int32), axis=2)
    n_vir = vir_irrep.shape[0]
    before = jnp.arange(n_vir)[:, None] < jnp.arange(n_vir)[None, :]
    first = jnp.sum(jnp.where(before[None], per[:, :, None], 0), axis=1)
    slot = jnp.arange(slots, dtype=jnp.int32)[None, None, :]
    offset = slot - first[:, :, None]
    hit = (offset >= 0) & (offset < per[:, :, None])
    place = jnp.sum(jnp.where(hit, offset * 8 + want[:, :, None], 0), axis=1)
    e_a = jnp.sum(jnp.where(hit, e_vir[None, :, None], 0.0), axis=1)
    earlier = jnp.arange(n_occ)[:, None] < jnp.arange(n_occ)[None, :]
    rank = jnp.sum((earlier & (occ_irrep[:, None] == occ_irrep[None, :])).astype(jnp.int32), axis=0)
    key = rank * 8 + occ_irrep
    e_i = jnp.sum(
        jnp.where(place[:, None, :] == key[None, :, None], e_occ[None, :, None], 0.0), axis=1
    )
    filled = slot[0] < jnp.array(counts, jnp.int32)[:, None]
    return jnp.where(filled, e_i - e_a, -1.0)


class Plan:
    def __init__(self, mesh, shape, counts):
        self.nr, self.nc = mesh.shape["row"], mesh.shape["col"]
        self.blocks, self.slots = shape[0], shape[2]
        self.own = self.slots // (self.nr * self.nc)
        self.panel = self.own * self.nc
        self.counts = counts
        self.depth = [-(-n // 128) * 128 for n in counts]
        self.width = [-(-k // (128 * self.nc)) * 128 for k in self.depth]


def barrier_line(plan, r, c):
    sem = pltpu.get_barrier_semaphore()
    for o in range(1, plan.nc):
        pl.semaphore_signal(
            sem, inc=1, device_id=(r, lax.rem(c + o, plan.nc)), device_id_type=MESH
        )
    for o in range(1, plan.nr):
        pl.semaphore_signal(
            sem, inc=1, device_id=(lax.rem(r + o, plan.nr), c), device_id_type=MESH
        )
    pl.semaphore_wait(sem, plan.nc + plan.nr - 2)


def remote(src, dst, send, recv, device):
    return pltpu.make_async_remote_copy(
        src_ref=src, dst_ref=dst, send_sem=send, recv_sem=recv, device_id=device, device_id_type=MESH
    )


class Spread:
    def __init__(self, plan, g, r, c, src, dst, base, send, recv, local):
        self.plan, self.g, self.r, self.c = plan, g, r, c
        self.src, self.dst, self.base = src, dst, base
        self.send, self.recv, self.local = send, recv, local

    def copy(self, o):
        p, g = self.plan, self.g
        to = lax.rem(self.c + o, p.nc)
        cols = pl.ds(pl.multiple_of(to * p.width[g], 128), p.width[g])
        rows = pl.ds(pl.multiple_of(self.base + self.c * p.own, p.own), p.own)
        return remote(
            self.src.at[g, :, cols], self.dst.at[rows, :],
            self.send.at[g, o], self.recv.at[g, o], (self.r, to),
        )

    def arrive(self, o):
        p, g = self.plan, self.g
        frm = lax.rem(self.c + p.nc - o, p.nc)
        rows = pl.ds(pl.multiple_of(self.base + frm * p.own, p.own), p.own)
        return remote(
            self.src.at[g, :, pl.ds(0, p.width[g])], self.dst.at[rows, :],
            self.send.at[g, o], self.recv.at[g, o], (self.r, lax.rem(self.c + o, p.nc)),
        ), self.alive(frm)

    def alive(self, col):
        return self.r * self.plan.nc + col < self.plan.depth[self.g] // self.plan.own

    def mine(self):
        p, g = self.plan, self.g
        cols = pl.ds(pl.multiple_of(self.c * p.width[g], 128), p.width[g])
        rows = pl.ds(pl.multiple_of(self.base + self.c * p.own, p.own), p.own)
        return pltpu.make_async_copy(
            self.src.at[g, :, cols], self.dst.at[rows, :], self.local.at[g]
        )

    def start(self):
        @pl.when(self.alive(self.c))
        def _():
            for o in range(1, self.plan.nc):
                self.copy(o).start()
            self.mine().start()

    def wait_recv(self):
        for o in range(1, self.plan.nc):
            copy, ok = self.arrive(o)
            pl.when(ok)(copy.wait_recv)
        pl.when(self.alive(self.c))(self.mine().wait)

    def wait_send(self):
        @pl.when(self.alive(self.c))
        def _():
            for o in range(1, self.plan.nc):
                self.copy(o).wait_send()


class Gather:
    def __init__(self, plan, g, r, c, src, dst, send, recv, fsend, frecv, local):
        self.plan, self.g, self.r, self.c = plan, g, r, c
        self.src, self.dst = src, dst
        self.send, self.recv, self.fsend, self.frecv = send, recv, fsend, frecv
        self.local = local
        self.twin = c + 1 - 2 * lax.rem(c, 2)

    def alive(self, col):
        return self.r * self.plan.nc + col < self.plan.depth[self.g] // self.plan.own

    def mine(self):
        return self.src.at[self.g, :, pl.ds(0, self.plan.depth[self.g])]

    def rows(self, col):
        p = self.plan
        return self.dst.at[pl.ds(pl.multiple_of(col * p.own, p.own), p.own), :]

    def copy(self, o):
        to = lax.rem(self.c + o, self.plan.nc)
        return remote(
            self.mine(), self.rows(self.c), self.send.at[self.g, o // 2],
            self.recv.at[self.g, o // 2], (self.r, to),
        )

    def arrive(self, o):
        frm = lax.rem(self.c + self.plan.nc - o, self.plan.nc)
        return remote(
            self.mine(), self.rows(frm), self.send.at[self.g, o // 2],
            self.recv.at[self.g, o // 2], (self.r, lax.rem(self.c + o, self.plan.nc)),
        ), frm

    def forward(self, o):
        frm = lax.rem(self.c + self.plan.nc - o, self.plan.nc)
        src = self.mine() if o == 0 else self.rows(frm)
        return remote(
            src, self.rows(frm), self.fsend.at[self.g, o // 2],
            self.frecv.at[self.g, o // 2], (self.r, self.twin),
        ), frm

    def from_twin(self, o):
        frm = lax.rem(self.twin + self.plan.nc - o, self.plan.nc)
        return remote(
            self.mine(), self.rows(frm), self.fsend.at[self.g, o // 2],
            self.frecv.at[self.g, o // 2], (self.r, self.twin),
        ), frm

    def own_copy(self):
        return pltpu.make_async_copy(self.mine(), self.rows(self.c), self.local.at[self.g])

    def start(self):
        @pl.when(self.alive(self.c))
        def _():
            for o in range(2, self.plan.nc, 2):
                self.copy(o).start()
            self.forward(0)[0].start()
            self.own_copy().start()

    def relay(self):
        for o in range(2, self.plan.nc, 2):
            copy, frm = self.arrive(o)
            forward, _ = self.forward(o)

            @pl.when(self.alive(frm))
            def _(copy=copy, forward=forward):
                copy.wait_recv()
                forward.start()

    def finish(self):
        for o in range(0, self.plan.nc, 2):
            copy, frm = self.from_twin(o)
            pl.when(self.alive(frm))(copy.wait_recv)
        for o in range(0, self.plan.nc, 2):
            forward, frm = self.forward(o)
            pl.when(self.alive(frm))(forward.wait_send)

        @pl.when(self.alive(self.c))
        def _():
            for o in range(2, self.plan.nc, 2):
                self.copy(o).wait_send()
            self.own_copy().wait()


class Stack:
    def __init__(self, plan, g, r, c, src, src_base, dst, send, recv):
        self.plan, self.g, self.r, self.c = plan, g, r, c
        self.src, self.src_base, self.dst = src, src_base, dst
        self.send, self.recv = send, recv
        self.full = plan.depth[g] // plan.panel
        self.rest = plan.depth[g] % plan.panel

    def copy(self, o, frm, size):
        p, g = self.plan, self.g
        at = pl.multiple_of(frm * p.panel, p.panel)
        return remote(
            self.src.at[pl.ds(self.src_base, size), :], self.dst.at[pl.ds(at, size), :],
            self.send.at[g, o], self.recv.at[g, o], (lax.rem(self.r + o, p.nr), self.c),
        )

    def cases(self, frm, act):
        if self.full:
            pl.when(frm < self.full)(lambda: act(frm, self.plan.panel))
        if self.rest:
            pl.when(frm == self.full)(lambda: act(self.full, self.rest))

    def start(self):
        def act(frm, size):
            for o in range(1, self.plan.nr):
                self.copy(o, frm, size).start()
        self.cases(self.r, act)

    def wait_send(self):
        def act(frm, size):
            for o in range(1, self.plan.nr):
                self.copy(o, frm, size).wait_send()
        self.cases(self.r, act)

    def wait_recv(self):
        for o in range(1, self.plan.nr):
            frm = lax.rem(self.r + self.plan.nr - o, self.plan.nr)
            self.cases(frm, lambda f, size, o=o: self.recv_one(o, f, size))

    def recv_one(self, o, frm, size):
        p, g = self.plan, self.g
        at = pl.multiple_of(frm * p.panel, p.panel)
        remote(
            self.dst.at[pl.ds(at, size), :], self.dst.at[pl.ds(at, size), :],
            self.send.at[g, o], self.recv.at[g, o], (lax.rem(self.r + o, p.nr), self.c),
        ).wait_recv()


def first_kernel(plan, t, w, v, *refs):
    n = plan.blocks
    tcol, vpan, wgrid = refs[:n], refs[n : 2 * n], refs[2 * n : 3 * n]
    ts, tr, ws, wr, gs, gr, fs, fr, zs, zr, loc_t, loc_w, loc_v = refs[3 * n :]
    r, c = lax.axis_index("row"), lax.axis_index("col")
    barrier_line(plan, r, c)
    base = r * plan.panel
    at = pl.multiple_of(base, plan.panel)
    t_spread = [Spread(plan, g, r, c, t, tcol[g], base, ts, tr, loc_t) for g in range(n)]
    w_spread = [Spread(plan, g, r, c, w, wgrid[g], 0, ws, wr, loc_w) for g in range(n)]
    v_gather = [Gather(plan, g, r, c, v, vpan[g], gs, gr, fs, fr, loc_v) for g in range(n)]
    stack = [Stack(plan, g, r, c, tcol[g], at, tcol[g], zs, zr) for g in range(n)]
    for g in range(n):
        t_spread[g].start()
    for g in range(n):
        v_gather[g].start()
    for g in range(n):
        w_spread[g].start()
    for g in range(n):
        t_spread[g].wait_recv()
        stack[g].start()
    for g in range(n):
        v_gather[g].relay()
    for g in range(n):
        v_gather[g].finish()
        w_spread[g].wait_recv()
        w_spread[g].wait_send()
        t_spread[g].wait_send()
    for g in range(n):
        stack[g].wait_recv()
        stack[g].wait_send()


def second_kernel(plan, t, *refs):
    n = plan.blocks
    x, tpan, xcol = refs[:n], refs[n : 2 * n], refs[2 * n : 3 * n]
    gs, gr, fs, fr, zs, zr, loc_t, loc_x = refs[3 * n :]
    r, c = lax.axis_index("row"), lax.axis_index("col")
    barrier_line(plan, r, c)
    gather = [Gather(plan, g, r, c, t, tpan[g], gs, gr, fs, fr, loc_t) for g in range(n)]
    stack = [Stack(plan, g, r, c, x[g], 0, xcol[g], zs, zr) for g in range(n)]

    def place(g, act):
        def one(frm, size):
            at = pl.multiple_of(frm * plan.panel, plan.panel)
            act(pltpu.make_async_copy(
                x[g].at[pl.ds(0, size), :], xcol[g].at[pl.ds(at, size), :], loc_x.at[g]
            ))
        stack[g].cases(r, one)

    for g in range(n):
        stack[g].start()
    for g in range(n):
        gather[g].start()
        place(g, lambda copy: copy.start())
    for g in range(n):
        gather[g].relay()
    for g in range(n):
        gather[g].finish()
        place(g, lambda copy: copy.wait())
    for g in range(n):
        stack[g].wait_recv()
        stack[g].wait_send()


def third_kernel(plan, *refs):
    n = plan.blocks
    z, zt = refs[:n], refs[n : 2 * n]
    rows, mirror = refs[2 * n : 2 * n + 2]
    rs, rr, ms, mr, loc_r, loc_m = refs[2 * n + 2 :]
    r, c = lax.axis_index("row"), lax.axis_index("col")
    sem = pltpu.get_barrier_semaphore()
    total = plan.nr * plan.nc
    me = r * plan.nc + c

    @pl.loop(1, total)
    def _(o):
        to = lax.rem(me + o, total)
        pl.semaphore_signal(
            sem, inc=1, device_id=(to // plan.nc, lax.rem(to, plan.nc)), device_id_type=MESH
        )
    pl.semaphore_wait(sem, total - 1)

    own, panel = plan.own, plan.panel

    def row_copy(g, o):
        to = lax.rem(c + o, plan.nc)
        src = z[g].at[pl.ds(pl.multiple_of(to * own, own), own), :]
        dst = rows.at[g, :, pl.ds(pl.multiple_of(c * plan.width[g], 128), plan.width[g])]
        if o == 0:
            return pltpu.make_async_copy(src, dst, loc_r.at[g])
        return remote(src, dst, rs.at[g, o], rr.at[g, o], (r, to))

    def row_arrival(g, o):
        frm = lax.rem(c + plan.nc - o, plan.nc)
        dst = rows.at[g, :, pl.ds(pl.multiple_of(frm * plan.width[g], 128), plan.width[g])]
        return remote(dst, dst, rs.at[g, o], rr.at[g, o], (r, lax.rem(c + o, plan.nc)))

    def mirror_copy(g, p, act_here, act_there):
        parts = plan.width[g] // own
        to = c * parts + p
        src = zt[g].at[pl.ds(p * own, own), :]
        dst = mirror.at[g, :, pl.ds(pl.multiple_of(r * panel, panel), panel)]

        @pl.when(to == me)
        def _():
            act_here(pltpu.make_async_copy(src, dst, loc_m.at[g]))

        @pl.when((to != me) & (to < total))
        def _():
            act_there(remote(
                src, dst, ms.at[g, p], mr.at[g, r], (to // plan.nc, lax.rem(to, plan.nc))
            ))

    def nothing(copy):
        return None

    def mirror_arrival(g, q):
        parts = plan.width[g] // own
        frm = q * plan.nc + me // parts
        dst = mirror.at[g, :, pl.ds(q * panel, panel)]

        @pl.when((frm != me) & (me // parts < plan.nc))
        def _():
            remote(dst, dst, ms.at[g, 0], mr.at[g, q], (lax.rem(r + 1, plan.nr), c)).wait_recv()

    for g in range(n):
        for p in range(plan.width[g] // own):
            mirror_copy(g, p, lambda copy: copy.start(), lambda copy: copy.start())
    for g in range(n):
        for o in range(plan.nc):
            row_copy(g, o).start()
    for g in range(n):
        for o in range(plan.nc):
            if o == 0:
                row_copy(g, o).wait()
            else:
                row_arrival(g, o).wait_recv()
                row_copy(g, o).wait_send()
        for q in range(plan.nr):
            mirror_arrival(g, q)
        for p in range(plan.width[g] // own):
            mirror_copy(g, p, lambda copy: copy.wait(), lambda copy: copy.wait_send())


def call(kernel, plan, outs, sems, number, *args):
    any_space = pl.BlockSpec(memory_space=pl.ANY)
    return pl.pallas_call(
        functools.partial(kernel, plan),
        out_shape=outs,
        in_specs=[any_space] * len(args),
        out_specs=[any_space] * len(outs),
        scratch_shapes=[pltpu.SemaphoreType.DMA(s) for s in sems],
        compiler_params=pltpu.CompilerParams(collective_id=number, has_side_effects=True),
    )(*args)


def body(mesh, t_amps, w_cycle, v_cycle, occ_irrep, vir_irrep, e_occ, e_vir):
    counts = block_counts(occ_irrep.shape[0], vir_irrep.shape[0], t_amps.shape[0])
    plan = Plan(mesh, t_amps.shape, counts)
    n, own, panel, nr, nc = plan.blocks, plan.own, plan.panel, plan.nr, plan.nc
    r = lax.axis_index("row")
    device = lax.axis_index(("row", "col"))
    limit = jnp.array(counts, jnp.int32)
    slot = jnp.arange(plan.slots, dtype=jnp.int32)
    my_slot = device * own + jnp.arange(own, dtype=jnp.int32)
    row_alive = my_slot[None, :] < limit[:, None]
    alive = slot[None, :] < limit[:, None]
    pair_energy = pair_table(occ_irrep, vir_irrep, e_occ, e_vir, counts, plan.slots)

    def half(*shape):
        return jax.ShapeDtypeStruct(shape, jnp.bfloat16)

    t_rows = jnp.where(row_alive[:, :, None], t_amps, jnp.zeros((), jnp.bfloat16))
    groups = range(n)
    column = [half(plan.depth[g], plan.width[g]) for g in groups]
    tile = [half(panel, plan.width[g]) for g in groups]
    rowpan = [half(panel, plan.depth[g]) for g in groups]
    plane, pair, line, one = (n, nc), (n, nc // 2), (n, nr), (n,)
    got = call(
        first_kernel, plan, column + rowpan + tile,
        [plane] * 4 + [pair] * 4 + [line] * 2 + [one] * 3, 1, t_rows, w_cycle, v_cycle,
    )
    tcol, vpan, wgrid = got[:n], got[n : 2 * n], got[2 * n :]
    panel_slot = r * panel + jnp.arange(panel, dtype=jnp.int32)
    x = []
    for g in groups:
        product = jnp.dot(vpan[g], tcol[g], preferred_element_type=jnp.float32)
        x_tile = (wgrid[g].astype(jnp.float32) + 0.5 * product).astype(jnp.bfloat16)
        x.append(jnp.where((panel_slot < counts[g])[:, None], x_tile, jnp.zeros((), jnp.bfloat16)))
    got = call(
        second_kernel, plan, rowpan + column, [pair] * 4 + [line] * 2 + [one] * 2, 2, t_rows, *x
    )
    tpan, xcol = got[:n], got[n:]
    z, zt = [], []
    for g in groups:
        z_tile = jnp.dot(tpan[g], xcol[g], preferred_element_type=jnp.float32).astype(jnp.bfloat16)
        z.append(z_tile)
        zt.append(z_tile.T)
    parts = max(plan.width) // own
    z_rows, z_mirror = call(
        third_kernel, plan, [half(n, own, plan.slots)] * 2,
        [plane] * 2 + [(n, parts), line] + [one] * 2, 3, *z, *zt,
    )
    row_energy = lax.dynamic_slice_in_dim(pair_energy, device * own, own, 1)
    denom = row_energy[:, :, None] + pair_energy[:, None, :]
    numer = v_cycle.astype(jnp.float32) + z_rows.astype(jnp.float32) + z_mirror.astype(jnp.float32)
    live = row_alive[:, :, None] & alive[:, None, :]
    return jnp.where(live, numer / denom, jnp.zeros((), jnp.float32))


def solution(mesh):
    rows = P(None, ("row", "col"), None)
    return jax.shard_map(
        functools.partial(body, mesh), mesh=mesh,
        in_specs=(rows, rows, rows, P(), P(), P(), P()), out_specs=rows, check_vma=False,
    )
```

time: 1290 us -> 783 us (0.61); the launches traced: 1290 us -> 767 us
  Pallas kernels: 0 us -> 693 us
  waiting for transfers between devices: 607 us -> 0 us
  local copies, waits for them, and re-layouts: 422 us -> 5.11 us
  blocking collectives: 160 us -> 0 us
  between operations: 13.5 us -> 0.28 us
    pallas_call x0 -> x3, Pallas kernels: none -> 693 us  [call(): pl.pallas_call(functools.partial(kernel, plan), out_shape=outs, in_specs=...]
    all_gather x4 -> x0, waiting for transfers between devices: 558 us -> none  [the longest x1 220 us: body(): lax.all_gather(x_grid, 'row', axis=1, tiled=True)]
    scatter x3 -> x0, local copies, waits for them, and re-layouts: 346 us -> none  [pair_table(): jnp.full((slots,), -1.0, jnp.float32).at[target].set(energy, mode='drop')]
    all_to_all x3 -> x0, blocking collectives: 160 us -> none  [the longest x1 54.1 us: body(): lax.all_to_all(tm, 'col', split_axis=2, concat_axis=1, tiled=True)]
    all_to_all x2 -> x0, waiting for transfers between devices: 48.2 us -> none  [the longest x1 48.2 us: body(): lax.all_to_all(z_grid.astype(jnp.bfloat16), 'col', split_axis=1, concat_a...]
    convert_element_type x7 -> x3, local copies, waits for them, and re-layouts: 33.1 us -> 4 us  [body(): jnp.dot(tpan[g], xcol[g], preferred_element_type=jnp.float32)]
    unnamed x15 -> x30, local copies, waits for them, and re-layouts: 21.6 us -> 1.1 us
    reduce_sum x1 -> x6, other arithmetic: 1.59 us -> 17.8 us  [the longest x1 9.07 us: pair_table(): place = jnp.sum(jnp.where(hit, offset * 8 + want[:, :, None], 0), axis=1)]
  transfers between devices with their start and end apart: 6 -> 0, of which waited for: 5 -> 0; matrix products, arithmetic and copies ran while one was open for 30% -> 0% of each run, Pallas kernels for 0% -> 0%
where the time goes in v1:
time: 783 us; the launch traced here: 767 us
  Pallas kernels  693 us (89%)
  matrix products  40.3 us (5%)
  other arithmetic  28.7 us (4%)
    pallas_call x3, Pallas kernels, call(): pl.pallas_call(functools.partial(kernel, plan), out_shape=outs, in_specs=...  693 us
    dot_general x3, matrix products, body(): jnp.dot(tpan[g], xcol[g], preferred_element_type=jnp.float32)  21.8 us
    dot_general x3, matrix products, body(): product = jnp.dot(vpan[g], tcol[g], preferred_element_type=jnp.float32)  18.6 us

profile of v1, /device:TPU:0, one launch (start us, length us, event | category | flops | bytes accessed | tf_op | source)
XLA Modules:
  0.0 767.4 jit_solution(17555370404916424437)
XLA Ops:
  0.0 0.7 broadcast_compare_fusion
  0.7 3.8 broadcast_select_fusion.t
  4.6 202.1 %shard_map.91 = (bf16[3584,512]{1,0:T(8,128)(2,1)}, bf16[2944,384]{1,0:T(8,128)(2,1)}, bf16[3328,512]{1,0:T(8,128)(2,1)}, bf16[1024,3584]{1,0:T(8,128)(2,1)}, bf...) custom-call(bf16[3,128,4096]{2,1,0:T(8,128)(2,1)} %broadcast_select_, ...), custom_call_target="tpu_custom_call" | custom-call | tf_op jit(solution)/shard_map/pallas_call | solution.py:411
  206.6 0.0 copy-start.9
  206.7 0.0 copy-start.11
  206.7 0.0 copy-start.13
  206.7 9.6 %fusion.3.refs_0_ = bf16[1024,512]{1,0:T(8,128)(2,1)} fusion(bf16[1024,3584]{1,0:T(8,128)(2,1)} %get-tuple-element.23, bf16[3584,512]{1,0:T(8,128)(2,1)} %get-tuple-element.24, bf16[1024,512]{1,0:T(8,128)(2,1)} %get-tuple-element.22, pred[1024]{0:T(1024)(128)(4,1)S(1)} %fusion.9), kind=kOutput, calls=%fused_computation.16 | convolution fusion | flops 3760717824 | bytes 13108224 | tf_op jit(solution)/shard_map/dot_general | solution.py:451
  216.3 0.0 copy-done.9
  216.3 0.0 copy-done.11
  216.3 0.0 copy-done.13
  216.3 0.0 copy-start.8
  216.3 0.0 copy-start.10
  216.3 0.0 copy-start.12
  216.3 4.3 fusion.5.refs_1_
  220.6 0.0 copy-done.8
  220.6 0.0 copy-done.10
  220.6 0.0 copy-done.12
  220.6 4.7 fusion.4.refs_2_
  225.3 250.4 %shard_map.92 = (bf16[1024,3584]{1,0:T(8,128)(2,1)}, bf16[1024,2944]{1,0:T(8,128)(2,1)}, bf16[1024,3328]{1,0:T(8,128)(2,1)}, bf16[3584,512]{1,0:T(8,128)(2,1)}, ...) custom-call(bf16[3,128,4096]{2,1,0:T(8,128)(2,1)} %broadcast_select_fusion.t, bf16[1024,512]{1,0:T(8,128)(2,1)} %fusion.3.refs_0_, ...), custom_call_target="tpu_custom_call" | custom-call | tf_op jit(solution)/shard_map/pallas_call | solution.py:411
  475.8 8.1 %convolution_convert_fusion = bf16[1024,512]{0,1:T(8,128)(2,1)S(1)} fusion(bf16[1024,3584]{1,0:T(8,128)(2,1)} %get-tuple-element.31, bf16[3584,512]{1,0:T(8,128)(2,1)} %get-tuple-element.32), kind=kOutput, calls=%fused_computation.13 | convolution fusion | flops 3758620672 | bytes 12058624 | tf_op jit(solution)/shard_map/dot_general | solution.py:460
  483.9 0.0 copy-start.1
  483.9 1.5 copy.19.refs_0_
  485.4 6.0 convolution_convert_fusion.2
  491.4 0.0 copy-done.1
  491.5 0.0 copy-start.3
  491.5 1.2 copy.20.refs_1_
  492.6 7.6 convolution_convert_fusion.1
  500.2 0.0 copy-done.3
  500.2 0.0 copy-start.2
  500.3 1.0 copy-done.2
  501.3 1.3 copy.21.refs_2_
  502.7 240.5 %shard_map.93 = (bf16[3,128,4096]{2,1,0:T(8,128)(2,1)}, bf16[3,128,4096]{2,1,0:T(8,128)(2,1)}) custom-call(bf16[1024,512]{1,0:T(8,128)(2,1)} %copy.19.refs_0_, bf16[1024,384]{1,0:T(8,128)(2,1)} %copy.20.refs_1_, bf16[1024,512]{1,0:T(8,128)(2,1)} %copy.21.refs_2_, bf16[512,1024]{1,0:T(8,128)(2,1)} %bitcast.15, bf16[384,1024]{1,0:T(8,128)(2,1)} %bitcast.17, ...), custom_call_target="tpu_custom_call" | custom-call | tf_op jit(solution)/shard_map/pallas_call | solution.py:411
  743.2 0.0 copy-done.5
  743.2 0.0 copy-done.7
  743.2 0.1 convert_reduce_fusion
  743.4 0.1 iota_compare_fusion
  743.5 0.4 select_reduce_fusion.2
  743.8 9.1 %select_reduce_fusion.1 = s32[3,4096]{1,0:T(4,128)S(1)} fusion(s32[3,500]{1,0:T(4,128)S(1)} %iota_xor_fusion, s32[3,500]{1,0:T(4,128)S(1)} %select_reduce_fusion.2, s32[3,500]{1,0:T(4,128)S(1)} %convert_reduce_fusion), kind=kLoop, calls=%fused_computation.1 | loop fusion | flops 49139712 | bytes 67152 | tf_op jit(solution)/shard_map/reduce_sum | solution.py:35
  752.9 0.1 convert_reduce_fusion.1
  753.0 0.0 copy-done.6
  753.0 0.4 select_reduce_fusion.3
  753.5 0.0 copy-done.14
  753.5 7.7 %select_reduce_fusion = f32[3,4096]{1,0:T(4,128)S(1)} fusion(f32[500]{0:T(512)S(1)} %copy-done.14, s32[3,500]{1,0:T(4,128)S(1)} %convert_reduce_fusion, s32[3,500]{1,0:T(4,128)S(1)} %select_reduce_fusion.2), kind=kLoop, calls=%fused_computation | loop fusion | flops 36851712 | bytes 63152 | tf_op jit(solution)/shard_map/reduce_sum | solution.py:36
  761.2 0.0 copy-done.4
  761.2 0.1 subtract_select_fusion
  761.3 0.1 iota_compare_fusion.1
  761.4 0.0 copy-done
  761.4 6.0 divide_select_fusion
  (12 shorter events, 0.0 us)
Async XLA Ops:
  206.6 9.7 %copy-start.9 = (bf16[1024,2944]{1,0:T(8,128)(2,1)S(1)}, bf16[1024,2944]{1,0:T(8,128)(2,1)}, u32[]{:S(2)}) copy-start(bf16[1024,2944]{1,0:T(8,128)(2,1)} %get-tuple-element.26) | copy-start | bytes 18087940
  206.7 9.6 %copy-start.11 = (bf16[2944,384]{1,0:T(8,128)(2,1)S(1)}, bf16[2944,384]{1,0:T(8,128)(2,1)}, u32[]{:S(2)}) copy-start(bf16[2944,384]{1,0:T(8,128)(2,1)} %get-tuple-element.27) | copy-start | bytes 6782980
  206.7 9.6 %copy-start.13 = (bf16[1024,384]{1,0:T(8,128)(2,1)S(1)}, bf16[1024,384]{1,0:T(8,128)(2,1)}, u32[]{:S(2)}) copy-start(bf16[1024,384]{1,0:T(8,128)(2,1)} %get-tuple-element.25) | copy-start | bytes 2359300
  216.3 4.3 copy-start.8
  216.3 4.3 copy-start.10
  216.3 4.3 copy-start.12
  483.9 7.6 copy-start.1
  491.5 8.8 %copy-start.3 = (bf16[1024,384]{0,1:T(8,128)(2,1)}, bf16[1024,384]{0,1:T(8,128)(2,1)S(1)}, u32[]{:S(2)}) copy-start(bf16[1024,384]{0,1:T(8,128)(2,1)S(1)} %convolution_convert_fusion.2) | copy-start | bytes 2359300
  500.2 1.0 copy-start.2
  501.3 241.9 %copy-start.5 = (s32[500]{0:T(512)S(1)}, s32[500]{0:T(512)}, u32[]{:S(2)}) copy-start(s32[500]{0:T(512)} %param.13) | copy-start | bytes 6004
  501.3 241.9 %copy-start.7 = (s32[50]{0:T(128)S(1)}, s32[50]{0:T(128)}, u32[]{:S(2)}) copy-start(s32[50]{0:T(128)} %param.12) | copy-start | bytes 604
  502.6 250.4 %copy-start.6 = (f32[50]{0:T(128)S(1)}, f32[50]{0:T(128)}, u32[]{:S(2)}) copy-start(f32[50]{0:T(128)} %param.14) | copy-start | bytes 604
  502.6 250.8 %copy-start.14 = (f32[500]{0:T(512)S(1)}, f32[500]{0:T(512)}, u32[]{:S(2)}) copy-start(f32[500]{0:T(512)} %param.15) | copy-start | bytes 6004
  502.6 258.6 %copy-start.4 = (s32[3]{0:T(128)S(1)}, s32[3]{0:T(128)}, u32[]{:S(2)}) copy-start(s32[3]{0:T(128)} %constant.13.clone) | copy-start | bytes 40
  502.6 258.8 %copy-start = (bf16[3,128,4096]{2,1,0:T(8,128)(2,1)S(1)}, bf16[3,128,4096]{2,1,0:T(8,128)(2,1)}, u32[]{:S(2)}) copy-start(bf16[3,128,4096]{2,1,0:T(8,128)(2,1)} %v.1) | copy-start | bytes 9437188

commit v2 on v1

--- a/solution.py
+++ b/solution.py
@@ -54,6 +54,12 @@
         self.depth = [-(-n // 128) * 128 for n in counts]
         self.width = [-(-k // (128 * self.nc)) * 128 for k in self.depth]
 
+    def planes(self, g):
+        return -(-self.depth[g] // self.panel)
+
+    def rows(self, g, s):
+        return min(self.panel, self.depth[g] - s * self.panel)
+
 
 def barrier_line(plan, r, c):
     sem = pltpu.get_barrier_semaphore()
@@ -80,54 +86,51 @@
         self.src, self.dst, self.base = src, dst, base
         self.send, self.recv, self.local = send, recv, local
 
-    def copy(self, o):
+    def rows(self, col):
+        p = self.plan
+        return pl.ds(pl.multiple_of(self.base + col * p.own, p.own), p.own)
+
+    def pieces(self, to):
         p, g = self.plan, self.g
-        to = lax.rem(self.c + o, p.nc)
-        cols = pl.ds(pl.multiple_of(to * p.width[g], 128), p.width[g])
-        rows = pl.ds(pl.multiple_of(self.base + self.c * p.own, p.own), p.own)
-        return remote(
-            self.src.at[g, :, cols], self.dst.at[rows, :],
-            self.send.at[g, o], self.recv.at[g, o], (self.r, to),
-        )
-
-    def arrive(self, o):
-        p, g = self.plan, self.g
-        frm = lax.rem(self.c + p.nc - o, p.nc)
-        rows = pl.ds(pl.multiple_of(self.base + frm * p.own, p.own), p.own)
-        return remote(
-            self.src.at[g, :, pl.ds(0, p.width[g])], self.dst.at[rows, :],
-            self.send.at[g, o], self.recv.at[g, o], (self.r, lax.rem(self.c + o, p.nc)),
-        ), self.alive(frm)
+        for b in range(p.width[g] // 128):
+            cols = pl.ds(pl.multiple_of((b * p.nc + to) * 128, 128), 128)
+            yield self.src.at[g, :, cols], self.dst.at[self.rows(self.c), pl.ds(b * 128, 128)]
+
+    def whole(self, o, col):
+        ref = self.dst.at[self.rows(col), :]
+        to = lax.rem(self.c + o, self.plan.nc)
+        return remote(ref, ref, self.send.at[self.g, o], self.recv.at[self.g, o], (self.r, to))
 
     def alive(self, col):
         return self.r * self.plan.nc + col < self.plan.depth[self.g] // self.plan.own
 
-    def mine(self):
-        p, g = self.plan, self.g
-        cols = pl.ds(pl.multiple_of(self.c * p.width[g], 128), p.width[g])
-        rows = pl.ds(pl.multiple_of(self.base + self.c * p.own, p.own), p.own)
-        return pltpu.make_async_copy(
-            self.src.at[g, :, cols], self.dst.at[rows, :], self.local.at[g]
-        )
-
     def start(self):
         @pl.when(self.alive(self.c))
         def _():
             for o in range(1, self.plan.nc):
-                self.copy(o).start()
-            self.mine().start()
+                to = lax.rem(self.c + o, self.plan.nc)
+                for src, dst in self.pieces(to):
+                    remote(
+                        src, dst, self.send.at[self.g, o], self.recv.at[self.g, o], (self.r, to)
+                    ).start()
+            for src, dst in self.pieces(self.c):
+                pltpu.make_async_copy(src, dst, self.local.at[self.g]).start()
 
     def wait_recv(self):
         for o in range(1, self.plan.nc):
-            copy, ok = self.arrive(o)
-            pl.when(ok)(copy.wait_recv)
-        pl.when(self.alive(self.c))(self.mine().wait)
+            frm = lax.rem(self.c + self.plan.nc - o, self.plan.nc)
+            pl.when(self.alive(frm))(self.whole(o, frm).wait_recv)
+
+        @pl.when(self.alive(self.c))
+        def _():
+            ref = self.dst.at[self.rows(self.c), :]
+            pltpu.make_async_copy(ref, ref, self.local.at[self.g]).wait()
 
     def wait_send(self):
         @pl.when(self.alive(self.c))
         def _():
             for o in range(1, self.plan.nc):
-                self.copy(o).wait_send()
+                self.whole(o, self.c).wait_send()
 
 
 class Gather:
@@ -214,51 +217,48 @@
 
 
 class Stack:
-    def __init__(self, plan, g, r, c, src, src_base, dst, send, recv):
+    def __init__(self, plan, g, r, c, src, dst, send, recv):
         self.plan, self.g, self.r, self.c = plan, g, r, c
-        self.src, self.src_base, self.dst = src, src_base, dst
-        self.send, self.recv = send, recv
-        self.full = plan.depth[g] // plan.panel
-        self.rest = plan.depth[g] % plan.panel
-
-    def copy(self, o, frm, size):
-        p, g = self.plan, self.g
-        at = pl.multiple_of(frm * p.panel, p.panel)
+        self.src, self.dst, self.send, self.recv = src, dst, send, recv
+        self.planes = plan.planes(g)
+
+    def rows(self, s):
+        return self.dst.at[pl.ds(s * self.plan.panel, self.plan.rows(self.g, s)), :]
+
+    def copy(self, s, up, first):
+        size = self.plan.rows(self.g, s)
+        src = self.src.at[pl.ds(0, size), :] if first and self.src is not None else self.rows(s)
+        to = lax.rem(self.r + (1 if up else self.plan.nr - 1), self.plan.nr)
         return remote(
-            self.src.at[pl.ds(self.src_base, size), :], self.dst.at[pl.ds(at, size), :],
-            self.send.at[g, o], self.recv.at[g, o], (lax.rem(self.r + o, p.nr), self.c),
+            src, self.rows(s), self.send.at[self.g, s, int(up)], self.recv.at[self.g, s],
+            (to, self.c),
         )
 
-    def cases(self, frm, act):
-        if self.full:
-            pl.when(frm < self.full)(lambda: act(frm, self.plan.panel))
-        if self.rest:
-            pl.when(frm == self.full)(lambda: act(self.full, self.rest))
+    def pass_on(self, r, s, act):
+        if r >= s and r + 1 < self.planes:
+            act(self.copy(s, True, r == s))
+        if r <= s and r > 0:
+            act(self.copy(s, False, r == s))
 
     def start(self):
-        def act(frm, size):
-            for o in range(1, self.plan.nr):
-                self.copy(o, frm, size).start()
-        self.cases(self.r, act)
+        for s in range(self.planes):
+            pl.when(self.r == s)(lambda s=s: self.pass_on(s, s, lambda copy: copy.start()))
+
+    def step(self, far):
+        for r in range(self.planes):
+            @pl.when(self.r == r)
+            def _(r=r):
+                for s in (r - far, r + far):
+                    if 0 <= s < self.planes:
+                        self.copy(s, s > r, False).wait_recv()
+                        self.pass_on(r, s, lambda copy: copy.start())
 
     def wait_send(self):
-        def act(frm, size):
-            for o in range(1, self.plan.nr):
-                self.copy(o, frm, size).wait_send()
-        self.cases(self.r, act)
-
-    def wait_recv(self):
-        for o in range(1, self.plan.nr):
-            frm = lax.rem(self.r + self.plan.nr - o, self.plan.nr)
-            self.cases(frm, lambda f, size, o=o: self.recv_one(o, f, size))
-
-    def recv_one(self, o, frm, size):
-        p, g = self.plan, self.g
-        at = pl.multiple_of(frm * p.panel, p.panel)
-        remote(
-            self.dst.at[pl.ds(at, size), :], self.dst.at[pl.ds(at, size), :],
-            self.send.at[g, o], self.recv.at[g, o], (lax.rem(self.r + o, p.nr), self.c),
-        ).wait_recv()
+        for r in range(self.planes):
+            @pl.when(self.r == r)
+            def _(r=r):
+                for s in range(self.planes):
+                    self.pass_on(r, s, lambda copy: copy.wait_send())
 
 
 def first_kernel(plan, t, w, v, *refs):
@@ -268,29 +268,28 @@
     r, c = lax.axis_index("row"), lax.axis_index("col")
     barrier_line(plan, r, c)
     base = r * plan.panel
-    at = pl.multiple_of(base, plan.panel)
     t_spread = [Spread(plan, g, r, c, t, tcol[g], base, ts, tr, loc_t) for g in range(n)]
     w_spread = [Spread(plan, g, r, c, w, wgrid[g], 0, ws, wr, loc_w) for g in range(n)]
     v_gather = [Gather(plan, g, r, c, v, vpan[g], gs, gr, fs, fr, loc_v) for g in range(n)]
-    stack = [Stack(plan, g, r, c, tcol[g], at, tcol[g], zs, zr) for g in range(n)]
+    stack = [Stack(plan, g, r, c, None, tcol[g], zs, zr) for g in range(n)]
     for g in range(n):
         t_spread[g].start()
-    for g in range(n):
-        v_gather[g].start()
-    for g in range(n):
-        w_spread[g].start()
     for g in range(n):
         t_spread[g].wait_recv()
         stack[g].start()
-    for g in range(n):
-        v_gather[g].relay()
+        v_gather[g].start()
+    for g in range(n):
+        w_spread[g].start()
+    for far in range(1, plan.nr):
+        for g in range(n):
+            stack[g].step(far)
+            if far == min(2, plan.nr - 1):
+                v_gather[g].relay()
     for g in range(n):
         v_gather[g].finish()
         w_spread[g].wait_recv()
         w_spread[g].wait_send()
         t_spread[g].wait_send()
-    for g in range(n):
-        stack[g].wait_recv()
         stack[g].wait_send()
 
 
@@ -301,28 +300,30 @@
     r, c = lax.axis_index("row"), lax.axis_index("col")
     barrier_line(plan, r, c)
     gather = [Gather(plan, g, r, c, t, tpan[g], gs, gr, fs, fr, loc_t) for g in range(n)]
-    stack = [Stack(plan, g, r, c, x[g], 0, xcol[g], zs, zr) for g in range(n)]
+    stack = [Stack(plan, g, r, c, x[g], xcol[g], zs, zr) for g in range(n)]
 
     def place(g, act):
-        def one(frm, size):
-            at = pl.multiple_of(frm * plan.panel, plan.panel)
-            act(pltpu.make_async_copy(
-                x[g].at[pl.ds(0, size), :], xcol[g].at[pl.ds(at, size), :], loc_x.at[g]
-            ))
-        stack[g].cases(r, one)
+        for s in range(plan.planes(g)):
+            @pl.when(r == s)
+            def _(s=s):
+                size = plan.rows(g, s)
+                act(pltpu.make_async_copy(
+                    x[g].at[pl.ds(0, size), :], stack[g].rows(s), loc_x.at[g]
+                ))
 
     for g in range(n):
         stack[g].start()
     for g in range(n):
         gather[g].start()
         place(g, lambda copy: copy.start())
-    for g in range(n):
-        gather[g].relay()
+    for far in range(1, plan.nr):
+        for g in range(n):
+            stack[g].step(far)
+            if far == min(2, plan.nr - 1):
+                gather[g].relay()
     for g in range(n):
         gather[g].finish()
         place(g, lambda copy: copy.wait())
-    for g in range(n):
-        stack[g].wait_recv()
         stack[g].wait_send()
 
 
@@ -332,78 +333,88 @@
     rows, mirror = refs[2 * n : 2 * n + 2]
     rs, rr, ms, mr, loc_r, loc_m = refs[2 * n + 2 :]
     r, c = lax.axis_index("row"), lax.axis_index("col")
-    sem = pltpu.get_barrier_semaphore()
-    total = plan.nr * plan.nc
-    me = r * plan.nc + c
-
-    @pl.loop(1, total)
-    def _(o):
-        to = lax.rem(me + o, total)
-        pl.semaphore_signal(
-            sem, inc=1, device_id=(to // plan.nc, lax.rem(to, plan.nc)), device_id_type=MESH
-        )
-    pl.semaphore_wait(sem, total - 1)
-
-    own, panel = plan.own, plan.panel
-
-    def row_copy(g, o):
-        to = lax.rem(c + o, plan.nc)
-        src = z[g].at[pl.ds(pl.multiple_of(to * own, own), own), :]
-        dst = rows.at[g, :, pl.ds(pl.multiple_of(c * plan.width[g], 128), plan.width[g])]
-        if o == 0:
-            return pltpu.make_async_copy(src, dst, loc_r.at[g])
-        return remote(src, dst, rs.at[g, o], rr.at[g, o], (r, to))
-
-    def row_arrival(g, o):
-        frm = lax.rem(c + plan.nc - o, plan.nc)
-        dst = rows.at[g, :, pl.ds(pl.multiple_of(frm * plan.width[g], 128), plan.width[g])]
-        return remote(dst, dst, rs.at[g, o], rr.at[g, o], (r, lax.rem(c + o, plan.nc)))
-
-    def mirror_copy(g, p, act_here, act_there):
-        parts = plan.width[g] // own
-        to = c * parts + p
-        src = zt[g].at[pl.ds(p * own, own), :]
-        dst = mirror.at[g, :, pl.ds(pl.multiple_of(r * panel, panel), panel)]
-
-        @pl.when(to == me)
-        def _():
-            act_here(pltpu.make_async_copy(src, dst, loc_m.at[g]))
-
-        @pl.when((to != me) & (to < total))
-        def _():
-            act_there(remote(
-                src, dst, ms.at[g, p], mr.at[g, r], (to // plan.nc, lax.rem(to, plan.nc))
-            ))
-
-    def nothing(copy):
-        return None
-
-    def mirror_arrival(g, q):
-        parts = plan.width[g] // own
-        frm = q * plan.nc + me // parts
-        dst = mirror.at[g, :, pl.ds(q * panel, panel)]
-
-        @pl.when((frm != me) & (me // parts < plan.nc))
-        def _():
-            remote(dst, dst, ms.at[g, 0], mr.at[g, q], (lax.rem(r + 1, plan.nr), c)).wait_recv()
-
-    for g in range(n):
-        for p in range(plan.width[g] // own):
-            mirror_copy(g, p, lambda copy: copy.start(), lambda copy: copy.start())
-    for g in range(n):
-        for o in range(plan.nc):
-            row_copy(g, o).start()
-    for g in range(n):
-        for o in range(plan.nc):
-            if o == 0:
-                row_copy(g, o).wait()
-            else:
-                row_arrival(g, o).wait_recv()
-                row_copy(g, o).wait_send()
-        for q in range(plan.nr):
-            mirror_arrival(g, q)
-        for p in range(plan.width[g] // own):
-            mirror_copy(g, p, lambda copy: copy.wait(), lambda copy: copy.wait_send())
+    own, panel, nr, nc = plan.own, plan.panel, plan.nr, plan.nc
+    total, sub = nr * nc, 128 // own
+    me = r * nc + c
+    if sub == 1:
+        barrier_line(plan, r, c)
+    else:
+        sem = pltpu.get_barrier_semaphore()
+
+        @pl.loop(1, total)
+        def _(o):
+            to = lax.rem(me + o, total)
+            pl.semaphore_signal(
+                sem, inc=1, device_id=(to // nc, lax.rem(to, nc)), device_id_type=MESH
+            )
+        pl.semaphore_wait(sem, total - 1)
+
+    def row_pieces(g, to):
+        for b in range(plan.width[g] // 128):
+            src = z[g].at[pl.ds(pl.multiple_of(to * own, own), own), pl.ds(b * 128, 128)]
+            yield src, rows.at[g, :, pl.ds(pl.multiple_of((b * nc + c) * 128, 128), 128)]
+
+    def row_alive(g, col):
+        return r * nc + col < plan.depth[g] // own
+
+    def row_whole(g, o):
+        ref = rows.at[g, :, pl.ds(0, plan.width[g])]
+        return remote(ref, ref, rs.at[g, o], rr.at[g, o], (r, lax.rem(c + o, nc)))
+
+    def start_rows(g):
+        for o in range(nc):
+            to = lax.rem(c + o, nc)
+
+            @pl.when(row_alive(g, to))
+            def _(o=o, to=to):
+                for src, dst in row_pieces(g, to):
+                    if o:
+                        remote(src, dst, rs.at[g, o], rr.at[g, o], (r, to)).start()
+                    else:
+                        pltpu.make_async_copy(src, dst, loc_r.at[g]).start()
+
+    def end_rows(g):
+        @pl.when(row_alive(g, c))
+        def _():
+            for o in range(1, nc):
+                row_whole(g, o).wait_recv()
+            ref = rows.at[g, :, pl.ds(0, plan.width[g])]
+            pltpu.make_async_copy(ref, ref, loc_r.at[g]).wait()
+        for o in range(1, nc):
+            pl.when(row_alive(g, lax.rem(c + o, nc)))(row_whole(g, o).wait_send)
+
+    def mirror_copies(g, here, there):
+        for s in range(plan.planes(g)):
+            @pl.when(r == s)
+            def _(s=s):
+                size = plan.rows(g, s)
+                for p in range(plan.width[g] // own):
+                    to = ((p // sub) * nc + c) * sub + p % sub
+                    src = zt[g].at[pl.ds(p * own, own), pl.ds(0, size)]
+                    dst = mirror.at[g, :, pl.ds(s * panel, size)]
+                    far = remote(
+                        src, dst, ms.at[g, p], mr.at[g, s], (to // nc, lax.rem(to, nc))
+                    )
+                    near = pltpu.make_async_copy(src, dst, loc_m.at[g])
+                    fits = to < plan.depth[g] // own
+                    pl.when((to == me) & fits)(functools.partial(here, near))
+                    pl.when((to != me) & fits)(functools.partial(there, far))
+
+    def mirror_arrivals(g):
+        for s in range(plan.planes(g)):
+            frm = s * nc + lax.rem(me // sub, nc)
+            dst = mirror.at[g, :, pl.ds(s * panel, plan.rows(g, s))]
+            copy = remote(dst, dst, ms.at[g, 0], mr.at[g, s], (lax.rem(r + 1, nr), c))
+            pl.when((frm != me) & (me < plan.depth[g] // own))(copy.wait_recv)
+
+    for g in range(n):
+        mirror_copies(g, lambda copy: copy.start(), lambda copy: copy.start())
+    for g in range(n):
+        start_rows(g)
+    for g in range(n):
+        end_rows(g)
+        mirror_arrivals(g)
+        mirror_copies(g, lambda copy: copy.wait(), lambda copy: copy.wait_send())
 
 
 def call(kernel, plan, outs, sems, number, *args):
@@ -440,9 +451,10 @@
     tile = [half(panel, plan.width[g]) for g in groups]
     rowpan = [half(panel, plan.depth[g]) for g in groups]
     plane, pair, line, one = (n, nc), (n, nc // 2), (n, nr), (n,)
+    both = (n, nr, 2)
     got = call(
         first_kernel, plan, column + rowpan + tile,
-        [plane] * 4 + [pair] * 4 + [line] * 2 + [one] * 3, 1, t_rows, w_cycle, v_cycle,
+        [plane] * 4 + [pair] * 4 + [both, line] + [one] * 3, 1, t_rows, w_cycle, v_cycle,
     )
     tcol, vpan, wgrid = got[:n], got[n : 2 * n], got[2 * n :]
     panel_slot = r * panel + jnp.arange(panel, dtype=jnp.int32)
@@ -452,7 +464,7 @@
         x_tile = (wgrid[g].astype(jnp.float32) + 0.5 * product).astype(jnp.bfloat16)
         x.append(jnp.where((panel_slot < counts[g])[:, None], x_tile, jnp.zeros((), jnp.bfloat16)))
     got = call(
-        second_kernel, plan, rowpan + column, [pair] * 4 + [line] * 2 + [one] * 2, 2, t_rows, *x
+        second_kernel, plan, rowpan + column, [pair] * 4 + [both, line] + [one] * 2, 2, t_rows, *x
     )
     tpan, xcol = got[:n], got[n:]
     z, zt = [], []

time: 783 us -> 478 us (0.61)
  the two profiles are of different devices: /device:TPU:0 before, /device:TPU:24 now
where the time goes in v2:
time: 478 us
  Pallas kernels  404 us (85%)
  matrix products  40.3 us (8%)
  other arithmetic  28.9 us (6%)
  local copies, waits for them, and re-layouts  5.11 us (1%)
    pallas_call x3, Pallas kernels, call(): pl.pallas_call(functools.partial(kernel, plan), out_shape=outs, in_specs=...  404 us
    dot_general x3, matrix products, body(): jnp.dot(tpan[g], xcol[g], preferred_element_type=jnp.float32)  21.8 us
    dot_general x3, matrix products, body(): product = jnp.dot(vpan[g], tcol[g], preferred_element_type=jnp.float32)  18.6 us

profile of v2, /device:TPU:24, one launch (start us, length us, event | category | flops | bytes accessed | tf_op | source)
XLA Modules:
  0.0 478.3 jit_solution(800397390204375445)
XLA Ops:
  0.0 0.7 broadcast_compare_fusion
  0.7 3.8 broadcast_select_fusion.t
  4.6 160.7 %shard_map.91 = (bf16[3584,512]{1,0:T(8,128)(2,1)}, bf16[2944,384]{1,0:T(8,128)(2,1)}, bf16[3328,512]{1,0:T(8,128)(2,1)}, bf16[1024,3584]{1,0:T(8,128)(2,1)}, bf...) custom-call(bf16[3,128,4096]{2,1,0:T(8,128)(2,1)} %broadcast_select_, ...), custom_call_target="tpu_custom_call" | custom-call | tf_op jit(solution)/shard_map/pallas_call | solution.py:422
  165.3 0.0 copy-start.9
  165.3 0.0 copy-start.11
  165.3 0.0 copy-start.13
  165.3 9.6 %fusion.3.refs_0_ = bf16[1024,512]{1,0:T(8,128)(2,1)} fusion(bf16[1024,3584]{1,0:T(8,128)(2,1)} %get-tuple-element.23, bf16[3584,512]{1,0:T(8,128)(2,1)} %get-tuple-element.24, bf16[1024,512]{1,0:T(8,128)(2,1)} %get-tuple-element.22, pred[1024]{0:T(1024)(128)(4,1)S(1)} %fusion.9), kind=kOutput, calls=%fused_computation.16 | convolution fusion | flops 3760717824 | bytes 13108224 | tf_op jit(solution)/shard_map/dot_general | solution.py:463
  174.9 0.0 copy-done.9
  175.0 0.0 copy-done.11
  175.0 0.0 copy-done.13
  175.0 0.0 copy-start.8
  175.0 0.0 copy-start.10
  175.0 0.0 copy-start.12
  175.0 4.3 fusion.5.refs_1_
  179.3 0.0 copy-done.8
  179.3 0.0 copy-done.10
  179.3 0.0 copy-done.12
  179.3 4.7 fusion.4.refs_2_
  184.0 167.4 %shard_map.92 = (bf16[1024,3584]{1,0:T(8,128)(2,1)}, bf16[1024,2944]{1,0:T(8,128)(2,1)}, bf16[1024,3328]{1,0:T(8,128)(2,1)}, bf16[3584,512]{1,0:T(8,128)(2,1)}, ...) custom-call(bf16[3,128,4096]{2,1,0:T(8,128)(2,1)} %broadcast_select_fusion.t, bf16[1024,512]{1,0:T(8,128)(2,1)} %fusion.3.refs_0_, ...), custom_call_target="tpu_custom_call" | custom-call | tf_op jit(solution)/shard_map/pallas_call | solution.py:422
  351.3 8.1 %convolution_convert_fusion = bf16[1024,512]{0,1:T(8,128)(2,1)S(1)} fusion(bf16[1024,3584]{1,0:T(8,128)(2,1)} %get-tuple-element.31, bf16[3584,512]{1,0:T(8,128)(2,1)} %get-tuple-element.32), kind=kOutput, calls=%fused_computation.13 | convolution fusion | flops 3758620672 | bytes 12058624 | tf_op jit(solution)/shard_map/dot_general | solution.py:472
  359.5 0.0 copy-start.1
  359.5 1.5 copy.19.refs_0_
  361.0 6.0 %convolution_convert_fusion.2 = bf16[1024,384]{0,1:T(8,128)(2,1)S(1)} fusion(bf16[1024,2944]{1,0:T(8,128)(2,1)} %get-tuple-element.33, bf16[2944,384]{1,0:T(8,128)(2,1)} %get-tuple-element.34), kind=kOutput, calls=%fused_computation.15 | convolution fusion | flops 2315649024 | bytes 9076736 | tf_op jit(solution)/shard_map/dot_general | solution.py:472
  367.0 0.0 copy-done.1
  367.0 0.0 copy-start.3
  367.0 1.2 copy.20.refs_1_
  368.2 7.6 %convolution_convert_fusion.1 = bf16[1024,512]{0,1:T(8,128)(2,1)S(1)} fusion(bf16[1024,3328]{1,0:T(8,128)(2,1)} %get-tuple-element.35, bf16[3328,512]{1,0:T(8,128)(2,1)} %get-tuple-element.36), kind=kOutput, calls=%fused_computation.14 | convolution fusion | flops 3490185216 | bytes 11272192 | tf_op jit(solution)/shard_map/dot_general | solution.py:472
  375.8 0.0 copy-done.3
  375.8 0.0 copy-start.2
  375.8 1.0 copy-done.2
  376.9 1.3 copy.21.refs_2_
  378.2 75.6 %shard_map.93 = (bf16[3,128,4096]{2,1,0:T(8,128)(2,1)}, bf16[3,128,4096]{2,1,0:T(8,128)(2,1)}) custom-call(bf16[1024,512]{1,0:T(8,128)(2,1)} %copy.19.refs_0_, bf16[1024,384]{1,0:T(8,128)(2,1)} %copy.20.refs_1_, bf16[1024,512]{1,0:T(8,128)(2,1)} %copy.21.refs_2_, bf16[512,1024]{1,0:T(8,128)(2,1)} %bitcast.15, bf16[384,1024]{1,0:T(8,128)(2,1)} %bitcast.17, ...), custom_call_target="tpu_custom_call" | custom-call | tf_op jit(solution)/shard_map/pallas_call | solution.py:422
  453.8 0.0 copy-done.5
  453.9 0.0 copy-done.7
  453.9 0.1 convert_reduce_fusion
  454.0 0.1 iota_compare_fusion
  454.1 0.4 select_reduce_fusion.2
  454.5 9.3 %select_reduce_fusion.1 = s32[3,4096]{1,0:T(4,128)S(1)} fusion(s32[3,500]{1,0:T(4,128)S(1)} %iota_xor_fusion, s32[3,500]{1,0:T(4,128)S(1)} %select_reduce_fusion.2, s32[3,500]{1,0:T(4,128)S(1)} %convert_reduce_fusion), kind=kLoop, calls=%fused_computation.1 | loop fusion | flops 49139712 | bytes 67152 | tf_op jit(solution)/shard_map/reduce_sum | solution.py:35
  463.8 0.1 convert_reduce_fusion.1
  463.9 0.0 copy-done.6
  463.9 0.4 select_reduce_fusion.3
  464.3 0.0 copy-done.14
  464.3 7.7 %select_reduce_fusion = f32[3,4096]{1,0:T(4,128)S(1)} fusion(f32[500]{0:T(512)S(1)} %copy-done.14, s32[3,500]{1,0:T(4,128)S(1)} %convert_reduce_fusion, s32[3,500]{1,0:T(4,128)S(1)} %select_reduce_fusion.2), kind=kLoop, calls=%fused_computation | loop fusion | flops 36851712 | bytes 63152 | tf_op jit(solution)/shard_map/reduce_sum | solution.py:36
  472.1 0.0 copy-done.4
  472.1 0.1 subtract_select_fusion
  472.2 0.1 iota_compare_fusion.1
  472.3 0.0 copy-done
  472.3 6.0 %divide_select_fusion = f32[3,128,4096]{2,1,0:T(8,128)} fusion(bf16[3,128,4096]{2,1,0:T(8,128)(2,1)} %get-tuple-element.38, bf16[3,128,4096]{2,1,0:T(8,128)(2,1)} %get-tuple-element.37, bf16[3,128,4096]{2,1,0:T(8,128)(2,1)S(1)} %copy-done, f32[3,4096]{1,0:T(4,128)S(1)} %subtract_select_fusion, f32[3,128]{1,0:T(4,128)S(1)} %constant_dynamic-slice_fusion, ...), kind=kLoop, calls=%fused_computation.6 | loop fusion | flops 14155776 | bytes 15792000 | tf_op jit(solution)/shard_map/jit(_where)/select_n | solution.py:484
  (12 shorter events, 0.0 us)
Async XLA Ops:
  165.3 9.6 %copy-start.9 = (bf16[1024,2944]{1,0:T(8,128)(2,1)S(1)}, bf16[1024,2944]{1,0:T(8,128)(2,1)}, u32[]{:S(2)}) copy-start(bf16[1024,2944]{1,0:T(8,128)(2,1)} %get-tuple-element.26) | copy-start | bytes 18087940
  165.3 9.6 %copy-start.11 = (bf16[2944,384]{1,0:T(8,128)(2,1)S(1)}, bf16[2944,384]{1,0:T(8,128)(2,1)}, u32[]{:S(2)}) copy-start(bf16[2944,384]{1,0:T(8,128)(2,1)} %get-tuple-element.27) | copy-start | bytes 6782980
  165.3 9.6 %copy-start.13 = (bf16[1024,384]{1,0:T(8,128)(2,1)S(1)}, bf16[1024,384]{1,0:T(8,128)(2,1)}, u32[]{:S(2)}) copy-start(bf16[1024,384]{1,0:T(8,128)(2,1)} %get-tuple-element.25) | copy-start | bytes 2359300
  175.0 4.3 copy-start.8
  175.0 4.3 copy-start.10
  175.0 4.3 copy-start.12
  359.5 7.6 %copy-start.1 = (bf16[1024,512]{0,1:T(8,128)(2,1)}, bf16[1024,512]{0,1:T(8,128)(2,1)S(1)}, u32[]{:S(2)}) copy-start(bf16[1024,512]{0,1:T(8,128)(2,1)S(1)} %convolution_convert_fusion) | copy-start | bytes 3145732
  367.0 8.8 %copy-start.3 = (bf16[1024,384]{0,1:T(8,128)(2,1)}, bf16[1024,384]{0,1:T(8,128)(2,1)S(1)}, u32[]{:S(2)}) copy-start(bf16[1024,384]{0,1:T(8,128)(2,1)S(1)} %convolution_convert_fusion.2) | copy-start | bytes 2359300
  375.8 1.0 copy-start.2
  376.9 77.0 %copy-start.5 = (s32[500]{0:T(512)S(1)}, s32[500]{0:T(512)}, u32[]{:S(2)}) copy-start(s32[500]{0:T(512)} %param.13) | copy-start | bytes 6004
  376.9 77.0 %copy-start.7 = (s32[50]{0:T(128)S(1)}, s32[50]{0:T(128)}, u32[]{:S(2)}) copy-start(s32[50]{0:T(128)} %param.12) | copy-start | bytes 604
  378.2 85.6 %copy-start.6 = (f32[50]{0:T(128)S(1)}, f32[50]{0:T(128)}, u32[]{:S(2)}) copy-start(f32[50]{0:T(128)} %param.14) | copy-start | bytes 604
  378.2 86.1 %copy-start.14 = (f32[500]{0:T(512)S(1)}, f32[500]{0:T(512)}, u32[]{:S(2)}) copy-start(f32[500]{0:T(512)} %param.15) | copy-start | bytes 6004
  378.2 93.8 %copy-start.4 = (s32[3]{0:T(128)S(1)}, s32[3]{0:T(128)}, u32[]{:S(2)}) copy-start(s32[3]{0:T(128)} %constant.13.clone) | copy-start | bytes 40
  378.2 94.0 %copy-start = (bf16[3,128,4096]{2,1,0:T(8,128)(2,1)S(1)}, bf16[3,128,4096]{2,1,0:T(8,128)(2,1)}, u32[]{:S(2)}) copy-start(bf16[3,128,4096]{2,1,0:T(8,128)(2,1)} %v.1) | copy-start | bytes 9437188

commit v3 on v2

--- a/solution.py
+++ b/solution.py
@@ -29,7 +29,7 @@
     n_vir = vir_irrep.shape[0]
     before = jnp.arange(n_vir)[:, None] < jnp.arange(n_vir)[None, :]
     first = jnp.sum(jnp.where(before[None], per[:, :, None], 0), axis=1)
-    slot = jnp.arange(slots, dtype=jnp.int32)[None, None, :]
+    slot = slots[None, None, :]
     offset = slot - first[:, :, None]
     hit = (offset >= 0) & (offset < per[:, :, None])
     place = jnp.sum(jnp.where(hit, offset * 8 + want[:, :, None], 0), axis=1)
@@ -54,6 +54,9 @@
         self.depth = [-(-n // 128) * 128 for n in counts]
         self.width = [-(-k // (128 * self.nc)) * 128 for k in self.depth]
 
+    def place(self, g, col):
+        return lax.rem(col + self.nc // 2, self.nc) if g % 3 == 2 else col
+
     def planes(self, g):
         return -(-self.depth[g] // self.panel)
 
@@ -61,7 +64,7 @@
         return min(self.panel, self.depth[g] - s * self.panel)
 
 
-def barrier_line(plan, r, c):
+def barrier_line(plan, r, c, across=0):
     sem = pltpu.get_barrier_semaphore()
     for o in range(1, plan.nc):
         pl.semaphore_signal(
@@ -71,7 +74,12 @@
         pl.semaphore_signal(
             sem, inc=1, device_id=(lax.rem(r + o, plan.nr), c), device_id_type=MESH
         )
-    pl.semaphore_wait(sem, plan.nc + plan.nr - 2)
+        if across:
+            pl.semaphore_signal(
+                sem, inc=1, device_id=(lax.rem(r + o, plan.nr), lax.rem(c + across, plan.nc)),
+                device_id_type=MESH,
+            )
+    pl.semaphore_wait(sem, plan.nc - 1 + (plan.nr - 1) * (2 if across else 1))
 
 
 def remote(src, dst, send, recv, device):
@@ -93,7 +101,7 @@
     def pieces(self, to):
         p, g = self.plan, self.g
         for b in range(p.width[g] // 128):
-            cols = pl.ds(pl.multiple_of((b * p.nc + to) * 128, 128), 128)
+            cols = pl.ds(pl.multiple_of((b * p.nc + p.place(g, to)) * 128, 128), 128)
             yield self.src.at[g, :, cols], self.dst.at[self.rows(self.c), pl.ds(b * 128, 128)]
 
     def whole(self, o, col):
@@ -223,11 +231,30 @@
         self.planes = plan.planes(g)
 
     def rows(self, s):
-        return self.dst.at[pl.ds(s * self.plan.panel, self.plan.rows(self.g, s)), :]
+        at = pl.ds(s * self.plan.panel, self.plan.rows(self.g, s))
+        return self.dst.at[at, pl.ds(0, self.live)]
+
+    def each_width(self, act):
+        p, width = self.plan, self.plan.width[self.g]
+        rest = p.depth[self.g] // 128 % p.nc
+        at = p.place(self.g, self.c)
+
+        def run(live):
+            self.live = live
+            act()
+
+        if rest:
+            pl.when(at < rest)(lambda: run(width))
+            if width > 128:
+                pl.when(at >= rest)(lambda: run(width - 128))
+        else:
+            run(width)
 
     def copy(self, s, up, first):
         size = self.plan.rows(self.g, s)
-        src = self.src.at[pl.ds(0, size), :] if first and self.src is not None else self.rows(s)
+        src = self.rows(s)
+        if first and self.src is not None:
+            src = self.src.at[pl.ds(0, size), pl.ds(0, self.live)]
         to = lax.rem(self.r + (1 if up else self.plan.nr - 1), self.plan.nr)
         return remote(
             src, self.rows(s), self.send.at[self.g, s, int(up)], self.recv.at[self.g, s],
@@ -241,10 +268,19 @@
             act(self.copy(s, False, r == s))
 
     def start(self):
+        self.each_width(self.start_one)
+
+    def step(self, far):
+        self.each_width(lambda: self.step_one(far))
+
+    def wait_send(self):
+        self.each_width(self.wait_send_one)
+
+    def start_one(self):
         for s in range(self.planes):
             pl.when(self.r == s)(lambda s=s: self.pass_on(s, s, lambda copy: copy.start()))
 
-    def step(self, far):
+    def step_one(self, far):
         for r in range(self.planes):
             @pl.when(self.r == r)
             def _(r=r):
@@ -253,7 +289,7 @@
                         self.copy(s, s > r, False).wait_recv()
                         self.pass_on(r, s, lambda copy: copy.start())
 
-    def wait_send(self):
+    def wait_send_one(self):
         for r in range(self.planes):
             @pl.when(self.r == r)
             def _(r=r):
@@ -308,7 +344,8 @@
             def _(s=s):
                 size = plan.rows(g, s)
                 act(pltpu.make_async_copy(
-                    x[g].at[pl.ds(0, size), :], stack[g].rows(s), loc_x.at[g]
+                    x[g].at[pl.ds(0, size), :], xcol[g].at[pl.ds(s * plan.panel, size), :],
+                    loc_x.at[g]
                 ))
 
     for g in range(n):
@@ -337,7 +374,7 @@
     total, sub = nr * nc, 128 // own
     me = r * nc + c
     if sub == 1:
-        barrier_line(plan, r, c)
+        barrier_line(plan, r, c, nc // 2)
     else:
         sem = pltpu.get_barrier_semaphore()
 
@@ -352,7 +389,7 @@
     def row_pieces(g, to):
         for b in range(plan.width[g] // 128):
             src = z[g].at[pl.ds(pl.multiple_of(to * own, own), own), pl.ds(b * 128, 128)]
-            yield src, rows.at[g, :, pl.ds(pl.multiple_of((b * nc + c) * 128, 128), 128)]
+            yield src, rows.at[g, :, pl.ds(pl.multiple_of((b * nc + plan.place(g, c)) * 128, 128), 128)]
 
     def row_alive(g, col):
         return r * nc + col < plan.depth[g] // own
@@ -389,7 +426,7 @@
             def _(s=s):
                 size = plan.rows(g, s)
                 for p in range(plan.width[g] // own):
-                    to = ((p // sub) * nc + c) * sub + p % sub
+                    to = ((p // sub) * nc + plan.place(g, c)) * sub + p % sub
                     src = zt[g].at[pl.ds(p * own, own), pl.ds(0, size)]
                     dst = mirror.at[g, :, pl.ds(s * panel, size)]
                     far = remote(
@@ -402,7 +439,7 @@
 
     def mirror_arrivals(g):
         for s in range(plan.planes(g)):
-            frm = s * nc + lax.rem(me // sub, nc)
+            frm = s * nc + plan.place(g, lax.rem(me // sub, nc))
             dst = mirror.at[g, :, pl.ds(s * panel, plan.rows(g, s))]
             copy = remote(dst, dst, ms.at[g, 0], mr.at[g, s], (lax.rem(r + 1, nr), c))
             pl.when((frm != me) & (me < plan.depth[g] // own))(copy.wait_recv)
@@ -440,7 +477,8 @@
     my_slot = device * own + jnp.arange(own, dtype=jnp.int32)
     row_alive = my_slot[None, :] < limit[:, None]
     alive = slot[None, :] < limit[:, None]
-    pair_energy = pair_table(occ_irrep, vir_irrep, e_occ, e_vir, counts, plan.slots)
+    row_energy = pair_table(occ_irrep, vir_irrep, e_occ, e_vir, counts, my_slot)
+    pair_energy = lax.all_gather(row_energy, ("row", "col"), axis=1, tiled=True)
 
     def half(*shape):
         return jax.ShapeDtypeStruct(shape, jnp.bfloat16)
@@ -477,7 +515,6 @@
         third_kernel, plan, [half(n, own, plan.slots)] * 2,
         [plane] * 2 + [(n, parts), line] + [one] * 2, 3, *z, *zt,
     )
-    row_energy = lax.dynamic_slice_in_dim(pair_energy, device * own, own, 1)
     denom = row_energy[:, :, None] + pair_energy[:, None, :]
     numer = v_cycle.astype(jnp.float32) + z_rows.astype(jnp.float32) + z_mirror.astype(jnp.float32)
     live = row_alive[:, :, None] & alive[:, None, :]

time: 478 us -> 495 us (1.036)
  the two profiles are of different devices: /device:TPU:24 before, /device:TPU:0 now
where the time goes in v3:
time: 495 us
  Pallas kernels  398 us (80%)
  matrix products  40.4 us (8%)
  blocking collectives  38.1 us (8%)
  other arithmetic  13.3 us (3%)
    pallas_call x3, Pallas kernels, call(): pl.pallas_call(functools.partial(kernel, plan), out_shape=outs, in_specs=...  398 us
    all_gather x1, blocking collectives, body(): pair_energy = lax.all_gather(row_energy, ('row', 'col'), axis=1, tiled=True)  38.1 us
    dot_general x3, matrix products, body(): jnp.dot(tpan[g], xcol[g], preferred_element_type=jnp.float32)  21.8 us
    dot_general x3, matrix products, body(): product = jnp.dot(vpan[g], tcol[g], preferred_element_type=jnp.float32)  18.6 us

profile of v3, /device:TPU:0, one launch (start us, length us, event | category | flops | bytes accessed | tf_op | source)
XLA Modules:
  0.0 495.3 jit_solution(4509614197650390820)
XLA Ops:
  0.0 0.7 broadcast_compare_fusion
  0.7 3.8 broadcast_select_fusion.t
  4.6 177.6 %shard_map.91 = (bf16[3584,512]{1,0:T(8,128)(2,1)}, bf16[2944,384]{1,0:T(8,128)(2,1)}, bf16[3328,512]{1,0:T(8,128)(2,1)}, bf16[1024,3584]{1,0:T(8,128)(2,1)}, bf...) custom-call(bf16[3,128,4096]{2,1,0:T(8,128)(2,1)} %broadcast_select_, ...), custom_call_target="tpu_custom_call" | custom-call | tf_op jit(solution)/shard_map/pallas_call | solution.py:459
  182.2 0.0 copy-start.10
  182.2 0.0 copy-start.12
  182.2 0.0 copy-start.14
  182.2 9.6 %fusion.refs_0_ = bf16[1024,512]{1,0:T(8,128)(2,1)} fusion(bf16[1024,3584]{1,0:T(8,128)(2,1)} %get-tuple-element.23, bf16[3584,512]{1,0:T(8,128)(2,1)} %get-tuple-element.24, bf16[1024,512]{1,0:T(8,128)(2,1)} %get-tuple-element.22, pred[1024]{0:T(1024)(128)(4,1)S(1)} %fusion.10), kind=kOutput, calls=%fused_computation.12 | convolution fusion | flops 3760717824 | bytes 13108224 | tf_op jit(solution)/shard_map/dot_general | solution.py:501
  191.9 0.0 copy-done.10
  191.9 0.0 copy-done.12
  191.9 0.0 copy-done.14
  191.9 0.0 copy-start.9
  191.9 0.0 copy-start.11
  191.9 0.0 copy-start.13
  191.9 4.3 fusion.2.refs_1_
  196.2 0.0 copy-done.9
  196.2 0.0 copy-done.11
  196.2 0.0 copy-done.13
  196.2 4.7 fusion.1.refs_2_
  200.9 168.3 %shard_map.92 = (bf16[1024,3584]{1,0:T(8,128)(2,1)}, bf16[1024,2944]{1,0:T(8,128)(2,1)}, bf16[1024,3328]{1,0:T(8,128)(2,1)}, bf16[3584,512]{1,0:T(8,128)(2,1)}, ...) custom-call(bf16[3,128,4096]{2,1,0:T(8,128)(2,1)} %broadcast_select_fusion.t, bf16[1024,512]{1,0:T(8,128)(2,1)} %fusion.refs_0_, ...), custom_call_target="tpu_custom_call" | custom-call | tf_op jit(solution)/shard_map/pallas_call | solution.py:459
  369.3 8.1 %convolution_convert_fusion = bf16[1024,512]{0,1:T(8,128)(2,1)S(1)} fusion(bf16[1024,3584]{1,0:T(8,128)(2,1)} %get-tuple-element.31, bf16[3584,512]{1,0:T(8,128)(2,1)} %get-tuple-element.32), kind=kOutput, calls=%fused_computation.6 | convolution fusion | flops 3758620672 | bytes 12058624 | tf_op jit(solution)/shard_map/dot_general | solution.py:510
  377.4 0.0 copy-start.1
  377.4 1.3 copy.19.refs_0_
  378.7 6.0 %convolution_convert_fusion.2 = bf16[1024,384]{0,1:T(8,128)(2,1)S(1)} fusion(bf16[1024,2944]{1,0:T(8,128)(2,1)} %get-tuple-element.33, bf16[2944,384]{1,0:T(8,128)(2,1)} %get-tuple-element.34), kind=kOutput, calls=%fused_computation.11 | convolution fusion | flops 2315649024 | bytes 9076736 | tf_op jit(solution)/shard_map/dot_general | solution.py:510
  384.8 0.0 copy-done.1
  384.8 0.0 copy-start.3
  384.8 1.2 copy.20.refs_1_
  385.9 7.6 %convolution_convert_fusion.1 = bf16[1024,512]{0,1:T(8,128)(2,1)S(1)} fusion(bf16[1024,3328]{1,0:T(8,128)(2,1)} %get-tuple-element.35, bf16[3328,512]{1,0:T(8,128)(2,1)} %get-tuple-element.36), kind=kOutput, calls=%fused_computation.7 | convolution fusion | flops 3490185216 | bytes 11272192 | tf_op jit(solution)/shard_map/dot_general | solution.py:510
  393.5 0.0 copy-done.3
  393.6 0.0 copy-start.2
  393.6 1.0 copy-done.2
  394.6 1.3 copy.21.refs_2_
  396.0 0.0 copy-start.4
  396.0 0.0 copy-start
  396.0 52.4 %shard_map.93 = (bf16[3,128,4096]{2,1,0:T(8,128)(2,1)}, bf16[3,128,4096]{2,1,0:T(8,128)(2,1)}) custom-call(bf16[1024,512]{1,0:T(8,128)(2,1)} %copy.19.refs_0_, bf16[1024,384]{1,0:T(8,128)(2,1)} %copy.20.refs_1_, bf16[1024,512]{1,0:T(8,128)(2,1)} %copy.21.refs_2_, bf16[512,1024]{1,0:T(8,128)(2,1)} %bitcast.15, bf16[384,1024]{1,0:T(8,128)(2,1)} %bitcast.17, ...), custom_call_target="tpu_custom_call" | custom-call | tf_op jit(solution)/shard_map/pallas_call | solution.py:459
  448.4 0.0 copy-done.5
  448.4 0.0 copy-done.7
  448.4 0.1 convert_reduce_fusion
  448.6 0.1 iota_compare_fusion
  448.6 0.4 select_reduce_fusion
  449.0 0.9 fusion.5
  449.9 0.1 convert_reduce_fusion.1
  450.0 0.0 copy-done.8
  450.0 0.1 select_reduce_fusion.2
  450.1 0.7 select_reduce_fusion.1
  450.8 0.1 subtract_select_fusion
  450.9 38.1 %all_gather.3 = f32[3,4096]{1,0:T(4,128)S(1)} all-gather(f32[3,128]{1,0:T(4,128)S(1)} %subtract_select_fusion), channel_id=1, replica_groups=mesh['row'=4,'col'=8] {'row','col'}, dimensions={1}, use_global_device_ids=true | all-gather | bytes 50688 | tf_op jit(solution)/shard_map/all_gather | solution.py:481
  488.9 0.1 iota_compare_fusion.1
  489.0 6.3 %divide_select_fusion = f32[3,128,4096]{2,1,0:T(8,128)} fusion(bf16[3,128,4096]{2,1,0:T(8,128)(2,1)} %get-tuple-element.38, bf16[3,128,4096]{2,1,0:T(8,128)(2,1)} %get-tuple-element.37, bf16[3,128,4096]{2,1,0:T(8,128)(2,1)S(1)} %copy-done, f32[3,4096]{1,0:T(4,128)S(1)} %all_gather.3, f32[3,128]{1,0:T(4,128)S(1)} %subtract_select_fusion, ...), kind=kLoop, calls=%fused_computation | loop fusion | flops 14155776 | bytes 15792000 | tf_op jit(solution)/shard_map/jit(_where)/select_n | solution.py:521
  (12 shorter events, 0.0 us)
Async XLA Ops:
  182.2 9.7 %copy-start.10 = (bf16[1024,2944]{1,0:T(8,128)(2,1)S(1)}, bf16[1024,2944]{1,0:T(8,128)(2,1)}, u32[]{:S(2)}) copy-start(bf16[1024,2944]{1,0:T(8,128)(2,1)} %get-tuple-element.26) | copy-start | bytes 18087940
  182.2 9.6 %copy-start.12 = (bf16[2944,384]{1,0:T(8,128)(2,1)S(1)}, bf16[2944,384]{1,0:T(8,128)(2,1)}, u32[]{:S(2)}) copy-start(bf16[2944,384]{1,0:T(8,128)(2,1)} %get-tuple-element.27) | copy-start | bytes 6782980
  182.2 9.6 %copy-start.14 = (bf16[1024,384]{1,0:T(8,128)(2,1)S(1)}, bf16[1024,384]{1,0:T(8,128)(2,1)}, u32[]{:S(2)}) copy-start(bf16[1024,384]{1,0:T(8,128)(2,1)} %get-tuple-element.25) | copy-start | bytes 2359300
  191.9 4.3 copy-start.9
  191.9 4.3 copy-start.11
  191.9 4.3 copy-start.13
  377.4 7.4 %copy-start.1 = (bf16[1024,512]{0,1:T(8,128)(2,1)}, bf16[1024,512]{0,1:T(8,128)(2,1)S(1)}, u32[]{:S(2)}) copy-start(bf16[1024,512]{0,1:T(8,128)(2,1)S(1)} %convolution_convert_fusion) | copy-start | bytes 3145732
  384.8 8.8 %copy-start.3 = (bf16[1024,384]{0,1:T(8,128)(2,1)}, bf16[1024,384]{0,1:T(8,128)(2,1)S(1)}, u32[]{:S(2)}) copy-start(bf16[1024,384]{0,1:T(8,128)(2,1)S(1)} %convolution_convert_fusion.2) | copy-start | bytes 2359300
  393.6 1.0 copy-start.2
  395.9 52.4 %copy-start.5 = (s32[500]{0:T(512)S(1)}, s32[500]{0:T(512)}, u32[]{:S(2)}) copy-start(s32[500]{0:T(512)} %param.13) | copy-start | bytes 6004
  396.0 52.5 %copy-start.7 = (s32[50]{0:T(128)S(1)}, s32[50]{0:T(128)}, u32[]{:S(2)}) copy-start(s32[50]{0:T(128)} %param.12) | copy-start | bytes 604
  396.0 54.0 %copy-start.8 = (f32[50]{0:T(128)S(1)}, f32[50]{0:T(128)}, u32[]{:S(2)}) copy-start(f32[50]{0:T(128)} %param.14) | copy-start | bytes 604
  396.0 54.1 %copy-start.6 = (f32[500]{0:T(512)S(1)}, f32[500]{0:T(512)}, u32[]{:S(2)}) copy-start(f32[500]{0:T(512)} %param.15) | copy-start | bytes 6004
  396.0 54.8 %copy-start.4 = (s32[3]{0:T(128)S(1)}, s32[3]{0:T(128)}, u32[]{:S(2)}) copy-start(s32[3]{0:T(128)} %constant.12.clone) | copy-start | bytes 40
  396.0 93.0 %copy-start = (bf16[3,128,4096]{2,1,0:T(8,128)(2,1)S(1)}, bf16[3,128,4096]{2,1,0:T(8,128)(2,1)}, u32[]{:S(2)}) copy-start(bf16[3,128,4096]{2,1,0:T(8,128)(2,1)} %v.1) | copy-start | bytes 9437188
